TPU v7x, 512 devices: a whole 4x8x8 slice. The times are simulated.
512 devices in a mesh: ctx: 32 (over y_lo, z), roll: 16 (over x, y_hi, core).
Axes of the slice: x: 4, y: 8 (y_hi: 2, y_lo: 4; y = y_hi * 4 + y_lo), z: 8, core: 2. Of those that a mesh axis runs over, the one named last changes fastest.
Arguments:
- block_order: int32 [32], replicated, may hold values from 0 to 31, as said below
- segment_ids: int32 [4096], replicated, may hold values from 0 to 3, as said below
- layer_input: bfloat16 [8192, 4096], P(None, 'ctx'), may hold values from -6 to 6
- query_states: bfloat16 [4096, 768], P('ctx')
- key_states: bfloat16 [4096, 128], P('ctx')
- value_states: bfloat16 [4096, 128], P('ctx'), may hold values from -6 to 6
- out_grad: bfloat16 [4096, 768], P('ctx'), may hold values from -24 to 24
- master_weight: float32 [8192, 128], P(('ctx', 'roll')), may hold values from -0.0625 to 0.0625
- first_moment: float32 [8192, 128], P(('ctx', 'roll')), may hold values from -60 to 60
- second_moment: float32 [8192, 128], P(('ctx', 'roll')), may hold values from 30 to 3000
Outputs:
- query_grad: bfloat16 [4096, 768], P('ctx')
- key_value_grad: bfloat16 [4096, 256], P('ctx')
- updated_master: float32 [8192, 128], P(('ctx', 'roll'))
- updated_first: float32 [8192, 128], P(('ctx', 'roll'))
- updated_second: float32 [8192, 128], P(('ctx', 'roll'))
- rollout_weight: bfloat16 [8192, 128], P('ctx')
Inputs may be any that keep to these rules, and one draw needn't show every extreme that they name: A permutation: index c of ctx holds the tokens at positions block_order[c] * 128 to block_order[c] * 128 + 127, in order; every block is held once. `segment_ids`: ids never fall along sequence positions; there are exactly 4 rollouts; no rollout begins at offset 128 // 2 of a block.
All inputs are finite; a program needn't handle non-finite values.
Results may differ from a plain program's by a relative error of at most 0.028.
Values may be sent and summed in bfloat16 or wider, within the bound.
A program may use at most 64 MiB of HBM per device.

v0:
```python
import math

import jax
import jax.numpy as jnp
from jax import lax
from jax.sharding import PartitionSpec as P

NEG_FILL = -1e30
BETA_ONE = 0.9
BETA_TWO = 0.95
ADAM_EPS = 1e-08
DECAY_RATE = 0.1
LEARN_RATE = 1e-06
CORRECT_ONE = 0.9999734386011124
CORRECT_TWO = 0.994079470779666


def sent_together(arrays, axis, dim, along):
    widths = [a.shape[along] for a in arrays]
    both = jnp.concatenate(arrays, axis=along)
    out = lax.all_gather(both, axis, axis=dim, tiled=True)
    return tuple(jnp.split(out, [sum(widths[:k]) for k in range(1, len(widths))], axis=along))


def from_everyone(array, axis):
    count = lax.axis_size(axis)
    return lax.all_to_all(
        jnp.broadcast_to(array[None], (count, *array.shape)), axis, 0, 0, tiled=True
    )


def gathered_once(array, axis):
    leaves = jax.tree.leaves(array)
    turns = sorted(range(len(leaves)), key=lambda k: -leaves[k].size)
    width = (1, *leaves[turns[0]].shape)[-1]
    lines = [
        jnp.pad(leaves[k].reshape(-1), (0, -leaves[k].size % width)).reshape(-1, width)
        for k in turns
    ]
    both, at, found = (from_everyone(jnp.concatenate(lines), axis), 0, {})
    for k, line in zip(turns, lines):
        piece = both[:, at : at + len(line)].reshape(len(both), -1)
        found[k] = piece[:, : leaves[k].size].reshape(-1, *leaves[k].shape)
        at += len(line)
    numbers = iter(range(len(leaves)))
    return jax.tree.map(lambda _: found[next(numbers)], array)


def folded_in_pairs(pieces, combine):
    while len(jax.tree.leaves(pieces)[0]) > 1:
        pieces = jax.vmap(combine)(
            *(jax.tree.map(lambda part: part[side::2], pieces) for side in (0, 1))
        )
    return jax.tree.map(lambda part: part[0], pieces)


def combined_all(array, axis, combine):
    pieces = gathered_once(array, axis)
    return folded_in_pairs(pieces, combine)


def cut_along(array, dim, count):
    lengths = array.shape
    blocks = array.reshape(*lengths[:dim], count, lengths[dim] // count, *lengths[dim + 1 :])
    return jnp.moveaxis(blocks, dim, 0)


def summed_on_arrival(array, axis, dim):
    blocks = cut_along(array, dim, lax.axis_size(axis))
    arrived = lax.all_to_all(blocks, axis, split_axis=0, concat_axis=0, tiled=True)
    return arrived.astype(jnp.float32).sum(axis=0)


def total_of_pieces(array, axis):
    blocks = lax.all_gather(array, axis).astype(jnp.float32)
    return blocks.sum(axis=0)


def in_order(blocks, dim):
    blocks = jnp.moveaxis(blocks, 0, dim)
    lengths = blocks.shape
    return blocks.reshape(*lengths[:dim], lengths[dim] * lengths[dim + 1], *lengths[dim + 2 :])


def gathered_copies(array, axis, dim):
    return in_order(from_everyone(array, axis), dim)


def contract_last(left_side, right_side):
    return lax.dot_general(
        left_side, right_side, (((1,), (1,)), ((), ())), preferred_element_type=jnp.float32
    )


def contract_first(left_side, right_side):
    return lax.dot_general(
        left_side, right_side, (((0,), (0,)), ((), ())), preferred_element_type=jnp.float32
    )


def visible_rows(q_pos, q_seg, key_pos, key_seg, head_group):
    visible = (key_pos[None, :] <= q_pos[:, None]) & (key_seg[None, :] == q_seg[:, None])
    return jnp.repeat(visible, head_group, axis=0)


def key_block_data(key_all, value_all, key_pos, key_seg):
    return (key_all, value_all, key_pos, key_seg)


def softmax_stats(
    q_rows, do_rows, key_all, value_all, key_pos, key_seg, q_pos, q_seg, head_group, score_scale
):
    block_width = math.gcd(key_all.shape[0], 512)
    row_total = q_rows.shape[0]

    def softmax_advance(step_index, carry):
        row_top, row_sum, weighted = carry
        key_block, value_block, pos_block, seg_block = key_block_data(
            key_all, value_all, key_pos, key_seg
        )
        visible = visible_rows(q_pos, q_seg, pos_block, seg_block, head_group)
        scores = jnp.where(visible, contract_last(q_rows, key_block) * score_scale, NEG_FILL)
        new_top = jnp.maximum(row_top, jnp.max(scores, axis=1))
        expo = jnp.where(visible, jnp.exp(scores - new_top[:, None]), 0.0)
        dprob = contract_last(do_rows, value_block)
        factor = jnp.exp(row_top - new_top)
        return (
            new_top,
            row_sum * factor + jnp.sum(expo, axis=1),
            weighted * factor + jnp.sum(expo * dprob, axis=1),
        )

    start_state = (
        jnp.full((row_total,), NEG_FILL, jnp.float32),
        jnp.zeros((row_total,), jnp.float32),
        jnp.zeros((row_total,), jnp.float32),
    )
    return lax.fori_loop(0, key_all.shape[0] // block_width, softmax_advance, start_state)


def gradient_pass(
    q_rows,
    do_rows,
    key_all,
    value_all,
    key_pos,
    key_seg,
    q_pos,
    q_seg,
    log_total,
    delta,
    head_group,
    score_scale,
):
    key_count, head_dim = key_all.shape
    block_width = math.gcd(key_count, 512)

    def gradient_advance(step_index, carry):
        query_acc, term = carry
        key_block, value_block, pos_block, seg_block = key_block_data(
            key_all, value_all, key_pos, key_seg
        )
        visible = visible_rows(q_pos, q_seg, pos_block, seg_block, head_group)
        scores = jnp.where(visible, contract_last(q_rows, key_block) * score_scale, NEG_FILL)
        weights = jnp.where(visible, jnp.exp(scores - log_total[:, None]), 0.0)
        dprob = contract_last(do_rows, value_block)
        dscore = weights * (dprob - delta[:, None])
        weights_half = weights.astype(jnp.bfloat16)
        dscore_half = dscore.astype(jnp.bfloat16)
        query_acc = query_acc + jnp.dot(dscore_half, key_block, preferred_element_type=jnp.float32)
        key_part = contract_first(dscore_half, q_rows) * score_scale
        value_part = contract_first(weights_half, do_rows)
        term = jnp.concatenate([key_part, value_part], axis=1)
        return (query_acc, term)

    start_state = (
        jnp.zeros((q_rows.shape[0], head_dim), jnp.float32),
        jnp.zeros((key_count, 2 * head_dim), jnp.float32),
    )
    return lax.fori_loop(0, key_count // block_width, gradient_advance, start_state)


def combine_stats(first_side, second_side):
    row_top = jnp.maximum(first_side[0], second_side[0])
    first_scale = jnp.exp(first_side[0] - row_top)
    second_scale = jnp.exp(second_side[0] - row_top)
    return (
        row_top,
        first_side[1] * first_scale + second_side[1] * second_scale,
        first_side[2] * first_scale + second_side[2] * second_scale,
    )


def body(
    block_order,
    segment_ids,
    layer_input,
    query_states,
    key_states,
    value_states,
    out_grad,
    master_weight,
    first_moment,
    second_moment,
):
    row_count, head_dim = key_states.shape
    head_group = query_states.shape[1] // head_dim
    ctx_count = lax.axis_size("ctx")
    roll_count = lax.axis_size("roll")
    ctx_rank = lax.axis_index("ctx")
    roll_rank = lax.axis_index("roll")
    score_scale = head_dim ** (-0.5)
    offsets = jnp.arange(row_count, dtype=jnp.int32)
    pos_table = block_order[:, None] * row_count + offsets[None, :]
    seg_table = segment_ids.reshape(ctx_count, row_count)
    q_pos = lax.dynamic_index_in_dim(pos_table, ctx_rank, 0, keepdims=False)
    q_seg = lax.dynamic_index_in_dim(seg_table, ctx_rank, 0, keepdims=False)
    q_rows = query_states.reshape(row_count * head_group, head_dim)
    do_rows = out_grad.reshape(row_count * head_group, head_dim)
    share_rows = row_count // roll_count
    first_row = roll_rank * share_rows
    key_all, value_all = sent_together(
        (
            lax.dynamic_slice_in_dim(key_states, first_row, share_rows, 0),
            lax.dynamic_slice_in_dim(value_states, first_row, share_rows, 0),
        ),
        "ctx",
        0,
        1,
    )
    key_pos = lax.dynamic_slice_in_dim(pos_table, first_row, share_rows, 1).reshape(-1)
    key_seg = lax.dynamic_slice_in_dim(seg_table, first_row, share_rows, 1).reshape(-1)
    part_top, part_sum, part_weighted = softmax_stats(
        q_rows, do_rows, key_all, value_all, key_pos, key_seg, q_pos, q_seg, head_group, score_scale
    )
    row_top, row_sum, weighted = combined_all(
        (part_top, part_sum, part_weighted), "roll", combine_stats
    )
    log_total = row_top + jnp.log(row_sum)
    delta = weighted / row_sum
    query_acc, term = gradient_pass(
        q_rows,
        do_rows,
        key_all,
        value_all,
        key_pos,
        key_seg,
        q_pos,
        q_seg,
        log_total,
        delta,
        head_group,
        score_scale,
    )
    key_value = summed_on_arrival(term.astype(jnp.bfloat16), "ctx", 0).astype(jnp.bfloat16)
    query_acc = total_of_pieces(query_acc.astype(jnp.bfloat16), "roll").astype(jnp.float32)
    key_value = gathered_copies(key_value, "roll", 0)
    query_grad = (
        (query_acc * score_scale).astype(jnp.bfloat16).reshape(row_count, head_group * head_dim)
    )
    key_grad = key_value[:, :head_dim]
    owner_rows = master_weight.shape[0]
    shard_grad = summed_on_arrival(
        jnp.dot(layer_input, key_grad, preferred_element_type=jnp.float32).astype(jnp.bfloat16),
        "ctx",
        0,
    )
    weight_grad = lax.dynamic_slice_in_dim(shard_grad, roll_rank * owner_rows, owner_rows, 0)
    updated_first = BETA_ONE * first_moment + (1.0 - BETA_ONE) * weight_grad
    updated_second = BETA_TWO * second_moment + (1.0 - BETA_TWO) * weight_grad * weight_grad
    update = (
        updated_first / CORRECT_ONE / (jnp.sqrt(updated_second / CORRECT_TWO) + ADAM_EPS)
        + DECAY_RATE * master_weight
    )
    updated_master = master_weight - LEARN_RATE * update
    rollout_weight = gathered_copies(updated_master.astype(jnp.bfloat16), "roll", 0)
    return (query_grad, key_value, updated_master, updated_first, updated_second, rollout_weight)


def solution(mesh):
    placed = (
        P(),
        P(),
        P(None, "ctx"),
        P("ctx", None),
        P("ctx", None),
        P("ctx", None),
        P("ctx", None),
        P(("ctx", "roll"), None),
        P(("ctx", "roll"), None),
        P(("ctx", "roll"), None),
    )
    return jax.shard_map(
        body,
        mesh=mesh,
        in_specs=placed,
        out_specs=(
            P("ctx", None),
            P("ctx", None),
            P(("ctx", "roll"), None),
            P(("ctx", "roll"), None),
            P(("ctx", "roll"), None),
            P("ctx", None),
        ),
        check_vma=False,
    )
```

profile of v0, /device:TPU:1, one launch (start us, length us, event | category | flops | bytes accessed | tf_op | source)
XLA Modules:
  0.0 259.2 jit_solution(6095639612398080479)
XLA Ops:
  7.2 0.8 broadcast_multiply_fusion
  8.1 0.7 fusion.19
  8.8 0.8 constant_dynamic-slice_fusion.4
  9.7 0.7 constant_dynamic-slice_fusion.1
  10.5 72.3 %all_gather.9 = bf16[256,256]{1,0:T(8,128)(2,1)S(1)} all-gather(bf16[8,256]{1,0:T(8,128)(2,1)S(1)} %pad_maximum_fusion.2), channel_id=1, replica_groups=mesh['ctx'=32,'roll'=16] {'ctx'}, dimensions={0}, use_global_device_ids=true | all-gather | bytes 135168 | tf_op jit(solution)/shard_map/all_gather | solution.py:21
  82.7 1.2 reshape.136
  83.9 1.9 reshape.137
  86.0 0.2 reshape.135
  86.2 0.3 copy.45
  86.5 0.3 fusion.25
  86.8 2.1 fusion.4
  88.9 0.7 broadcast_in_dim.65
  89.6 21.6 %all-to-all-start = ((f32[16,3,768]{2,1,0:T(4,128)}), f32[16,3,768]{2,1,0:T(4,128)S(1)}, u32[]{:S(2)}, u32[]{:S(2)}) async-start(f32[16,3,768]{2,1,0:T(4,128)} %broadcast_in_dim.65), calls=%async_computation | async-start | bytes 393216 | tf_op jit(solution)/shard_map/all_to_all | solution.py:27
  111.2 1.8 reshape.146
  113.0 8.8 %all-to-all-done = f32[16,3,768]{2,1,0:T(4,128)S(1)} async-done(((f32[16,3,768]{2,1,0:T(4,128)}), f32[16,3,768]{2,1,0:T(4,128)S(1)}, u32[]{:S(2)}, u32[]{:S(2)}) %all-to-all-start) | async-done | bytes 147488 | tf_op jit(solution)/shard_map/all_to_all | solution.py:27
  122.5 1.4 multiply_convert_fusion
  123.9 1.8 convolution_convert_fusion.1
  125.7 1.2 fusion.3
  126.9 1.2 convolution_convert_fusion.2
  128.1 14.2 %all_to_all.25 = bf16[32,8,256]{2,1,0:T(8,128)(2,1)S(1)} all-to-all(bf16[32,8,256]{2,1,0:T(8,128)(2,1)S(1)} %pad_maximum_fusion), channel_id=1, replica_groups=mesh['ctx'=32,'roll'=16] {'ctx'}, dimensions={0} | all-to-all | bytes 262144 | tf_op jit(solution)/shard_map/all_to_all | solution.py:70
  142.4 15.0 %all_to_all.26 = bf16[16,8,256]{2,1,0:T(8,128)(2,1)S(1)} all-to-all(bf16[16,8,256]{2,1,0:T(8,128)(2,1)S(1)} %broadcast_in_dim.66), channel_id=1, replica_groups=mesh['ctx'=32,'roll'=16] {'roll'}, dimensions={0} | all-to-all | bytes 131072 | tf_op jit(solution)/shard_map/all_to_all | solution.py:27
  157.4 0.7 convolution_convert_fusion
  158.2 1.6 copy.59
  159.8 4.8 %all-to-all-start.3 = ((bf16[32,256,128]{1,2,0:T(8,128)(2,1)}), bf16[32,256,128]{1,2,0:T(8,128)(2,1)}, u32[]{:S(2)}, u32[]{:S(2)}) async-start(bf16[32,256,128]{1,2,0:T(8,128)(2,1)} %bitcast.43), calls=%async_computation.3 | async-start | bytes 4194304 | tf_op jit(solution)/shard_map/all_to_all | solution.py:70
  164.6 62.1 %all-to-all-done.3 = bf16[32,256,128]{1,2,0:T(8,128)(2,1)} async-done(((bf16[32,256,128]{1,2,0:T(8,128)(2,1)}), bf16[32,256,128]{1,2,0:T(8,128)(2,1)}, u32[]{:S(2)}, u32[]{:S(2)}) %all-to-all-start.3) | async-done | bytes 2097184 | tf_op jit(solution)/shard_map/all_to_all | solution.py:70
  226.7 1.9 convert_reduce_fusion.1
  228.8 0.6 fusion.22
  229.4 18.4 %all_to_all.27 = bf16[16,16,128]{2,1,0:T(8,128)(2,1)S(1)} all-to-all(bf16[16,16,128]{2,1,0:T(8,128)(2,1)S(1)} %broadcast_in_dim.67), channel_id=1, replica_groups=mesh['ctx'=32,'roll'=16] {'roll'}, dimensions={0} | all-to-all | bytes 131072 | tf_op jit(solution)/shard_map/all_to_all | solution.py:27
  247.8 2.4 convert_reduce_fusion
  250.2 0.9 convert_element_type.41
  251.1 0.6 copy.69
  251.7 0.6 copy.70
  (61 shorter events, 1.5 us)
Async XLA Ops:
  7.2 150.3 %copy-start = (bf16[8192,128]{1,0:T(8,128)(2,1)S(1)}, bf16[8192,128]{1,0:T(8,128)(2,1)}, u32[]{:S(2)}) copy-start(bf16[8192,128]{1,0:T(8,128)(2,1)} %param.12) | copy-start | bytes 6291460
  82.7 6.1 %copy-start.2 = (bf16[256,256]{1,0:T(8,128)(2,1)}, bf16[256,256]{1,0:T(8,128)(2,1)S(1)}, u32[]{:S(2)}) copy-start(bf16[256,256]{1,0:T(8,128)(2,1)S(1)} %all_gather.9) | copy-start | bytes 393220
  83.9 5.0 %copy-start.1 = (bf16[768,128]{1,0:T(8,128)(2,1)}, bf16[768,128]{1,0:T(8,128)(2,1)S(1)}, u32[]{:S(2)}) copy-start(bf16[768,128]{1,0:T(8,128)(2,1)S(1)} %reshape.136) | copy-start | bytes 589828
  89.6 32.2 %all-to-all-start = ((f32[16,3,768]{2,1,0:T(4,128)}), f32[16,3,768]{2,1,0:T(4,128)S(1)}, u32[]{:S(2)}, u32[]{:S(2)}) async-start(f32[16,3,768]{2,1,0:T(4,128)} %broadcast_in_dim.65), calls=%async_computation | async-start | bytes 393216 | tf_op jit(solution)/shard_map/all_to_all | solution.py:27
  111.2 136.6 %all-gather.3.cloned.1.call-start = ((), (), s32[]{:S(2)}) async-start(), calls=%async_computation.5 | async-start | bytes 3342336 | tf_op jit(solution)/shard_map/all_gather | solution.py:75
  159.8 66.9 %all-to-all-start.3 = ((bf16[32,256,128]{1,2,0:T(8,128)(2,1)}), bf16[32,256,128]{1,2,0:T(8,128)(2,1)}, u32[]{:S(2)}, u32[]{:S(2)}) async-start(bf16[32,256,128]{1,2,0:T(8,128)(2,1)} %bitcast.43), calls=%async_computation.3 | async-start | bytes 4194304 | tf_op jit(solution)/shard_map/all_to_all | solution.py:70
  164.6 64.2 %copy-start.3 = (f32[16,128]{1,0:T(8,128)S(1)}, f32[16,128]{1,0:T(8,128)}, u32[]{:S(2)}) copy-start(f32[16,128]{1,0:T(8,128)} %param.17) | copy-start | bytes 24580
  164.6 64.2 %copy-start.4 = (f32[16,128]{1,0:T(8,128)S(1)}, f32[16,128]{1,0:T(8,128)}, u32[]{:S(2)}) copy-start(f32[16,128]{1,0:T(8,128)} %param.18) | copy-start | bytes 24580
  164.6 64.2 %copy-start.5 = (f32[16,128]{1,0:T(8,128)S(1)}, f32[16,128]{1,0:T(8,128)}, u32[]{:S(2)}) copy-start(f32[16,128]{1,0:T(8,128)} %param.19) | copy-start | bytes 24580
Sparse Core Ops, SparseCore 0:
  125.9 69.3 all-gather.2
where the time goes:
time: 261 us; the launch traced here: 259 us
  blocking collectives  120 us (46%)
  waiting for transfers between devices  70.9 us (27%)
  starting transfers between devices  26.4 us (10%)
  between operations  14.3 us (5%)
  local copies, waits for them, and re-layouts  12.9 us (5%)
  other arithmetic  7.5 us (3%)
  matrix products  7.32 us (3%)
    all_gather x1, blocking collectives, sent_together(): out = lax.all_gather(both, axis, axis=dim, tiled=True)  72.3 us
    all_to_all x1, waiting for transfers between devices, summed_on_arrival(): lax.all_to_all(blocks, axis, split_axis=0, concat_axis=0, tiled=True)  62.1 us
    all_to_all x2, blocking collectives, from_everyone(): lax.all_to_all(jnp.broadcast_to(array[None], (count, *array.shape)), axis...  33.4 us
    all_to_all x1, starting transfers between devices, from_everyone(): lax.all_to_all(jnp.broadcast_to(array[None], (count, *array.shape)), axis...  21.6 us
    all_to_all x1, blocking collectives, summed_on_arrival(): lax.all_to_all(blocks, axis, split_axis=0, concat_axis=0, tiled=True)  14.2 us
    all_to_all x1, waiting for transfers between devices, from_everyone(): lax.all_to_all(jnp.broadcast_to(array[None], (count, *array.shape)), axis...  8.75 us
  transfers between devices with their start and end apart: 3, of which 2 were waited for; matrix products, arithmetic and copies ran while one was open for 4% of the time, Pallas kernels for 0%

commit v1 on v0

v1 whole, which is shorter than its diff:
```python
import functools

import jax
import jax.numpy as jnp
from jax import lax
from jax.experimental import pallas as pl
from jax.experimental.pallas import tpu as pltpu
from jax.sharding import PartitionSpec as P

NEG_FILL = -1e30
BETA_ONE = 0.9
BETA_TWO = 0.95
ADAM_EPS = 1e-08
DECAY_RATE = 0.1
LEARN_RATE = 1e-06
CORRECT_ONE = 0.9999734386011124
CORRECT_TWO = 0.994079470779666

MESH = pl.DeviceIdType.MESH
SHARE = 8
OWN = 16
HEADS = 6
BF = jnp.bfloat16
F32 = jnp.float32

(LOAD, KV, STATS, DKV, DQ, DQALL, KVG, WG, ROLL, OUT) = range(10)


def push(axis, me, count, src, dst, send_sem, recv_sem):
    @pl.loop(1, count)
    def _(step):
        peer = lax.rem(me + step, count)
        pltpu.make_async_remote_copy(
            src_ref=src(peer),
            dst_ref=dst,
            send_sem=send_sem,
            recv_sem=recv_sem,
            device_id={axis: peer},
            device_id_type=MESH,
        ).start()


def drain(buf, count, sem):
    part = buf.at[pl.ds(0, count - 1)]
    pltpu.make_async_copy(part, part, sem).wait()


def contract(left, right, dims):
    return lax.dot_general(left, right, (dims, ((), ())), preferred_element_type=F32)


def kernel(
    ctx,
    roll,
    order_hbm,
    seg_hbm,
    x_hbm,
    q_hbm,
    k_hbm,
    v_hbm,
    do_hbm,
    mw_hbm,
    m1_hbm,
    m2_hbm,
    qg_out,
    kvg_out,
    mw_out,
    m1_out,
    m2_out,
    rw_out,
    order,
    seg,
    x_in,
    q_in,
    k_in,
    v_in,
    do_in,
    mw_in,
    m1_in,
    m2_in,
    kv_wide,
    bias,
    expo,
    dprob,
    kv,
    stats,
    dkv_to,
    dkv_from,
    dq_to,
    dq_from,
    dq_all,
    kvg,
    wg_to,
    wg_from,
    rolled,
    qg_stage,
    kvg_stage,
    mw_stage,
    m1_stage,
    m2_stage,
    load_sem,
    send_sem,
    recv_sem,
    out_sem,
):
    c = lax.axis_index("ctx")
    r = lax.axis_index("roll")
    rows = k_in.shape[0]
    hd = k_in.shape[1]
    keys = ctx * SHARE
    scale = hd**-0.5
    piece = HEADS * SHARE

    loads = [
        pltpu.make_async_copy(src, dst, load_sem.at[i])
        for i, (src, dst) in enumerate(
            (
                (k_hbm, k_in),
                (v_hbm, v_in),
                (order_hbm, order),
                (seg_hbm, seg),
                (q_hbm, q_in),
                (do_hbm, do_in),
                (x_hbm.at[:, r], x_in),
                (mw_hbm, mw_in),
                (m1_hbm, m1_in),
                (m2_hbm, m2_in),
            )
        )
    ]
    for load in loads:
        load.start()

    barrier = pltpu.get_barrier_semaphore()

    @pl.loop(1, ctx)
    def _(step):
        pl.semaphore_signal(
            barrier, inc=1, device_id={"ctx": lax.rem(c + step, ctx)}, device_id_type=MESH
        )

    @pl.loop(1, roll)
    def _(step):
        pl.semaphore_signal(
            barrier, inc=1, device_id={"roll": lax.rem(r + step, roll)}, device_id_type=MESH
        )

    loads[0].wait()
    loads[1].wait()
    kv_wide[0] = k_in[...].astype(F32)
    kv_wide[1] = v_in[...].astype(F32)
    first = pl.multiple_of(r * SHARE, SHARE)
    own = jnp.concatenate(
        [kv_wide[0, pl.ds(first, SHARE), :], kv_wide[1, pl.ds(first, SHARE), :]], axis=0
    )
    kv[c] = own.astype(BF)
    pl.semaphore_wait(barrier, ctx + roll - 2)
    push("ctx", c, ctx, lambda peer: kv.at[c], kv.at[c], send_sem.at[KV], recv_sem.at[KV])

    loads[2].wait()
    loads[3].wait()
    ids = seg[...]
    q_seg = seg[pl.ds(c, 1), :]
    lane = lax.broadcasted_iota(jnp.int32, (1, rows), 1)
    q_pos = order[c] * rows + lane
    start = jnp.zeros((1, rows), F32)
    for rollout in range(3):
        total = jnp.sum(jnp.where(ids == rollout, 1.0, 0.0), axis=0, keepdims=True)
        total = jnp.sum(total, axis=1, keepdims=True)
        start = start + jnp.where(q_seg > rollout, total, 0.0)
    start = start.astype(jnp.int32)
    sub = lax.broadcasted_iota(jnp.int32, (SHARE, rows), 0)
    latest = q_pos - sub - r * SHARE
    earliest = start - sub - r * SHARE
    for block in range(ctx):
        base = order[block] * rows
        seen = (latest >= base) & (earliest <= base)
        bias[pl.ds(block * SHARE, SHARE), :] = jnp.where(seen, 0.0, NEG_FILL)

    loads[4].wait()
    loads[5].wait()
    drain(kv, ctx, recv_sem.at[KV])
    wide = kv[...].astype(F32)
    key = wide[:, :SHARE, :].reshape(keys, hd).astype(BF)
    value = wide[:, SHARE:, :].reshape(keys, hd).astype(BF)
    tops, sums, weighteds = [], [], []
    for h in range(HEADS):
        cols = pl.ds(h * hd, hd)
        scores = contract(key, q_in[:, cols], ((1,), (1,))) * scale + bias[...]
        grads = contract(value, do_in[:, cols], ((1,), (1,)))
        top = jnp.max(scores, axis=0, keepdims=True)
        weights = jnp.exp(scores - top)
        expo[h] = weights
        dprob[h] = grads
        tops.append(top)
        sums.append(jnp.sum(weights, axis=0, keepdims=True))
        weighteds.append(jnp.sum(weights * grads, axis=0, keepdims=True))
    pad = jnp.zeros((8 - HEADS, rows), F32)
    for i, parts in enumerate((tops, sums, weighteds)):
        stats[r, i] = jnp.concatenate([*parts, pad], axis=0)
    push(
        "roll", r, roll, lambda peer: stats.at[r], stats.at[r], send_sem.at[STATS], recv_sem.at[STATS]
    )
    own_top = stats[r, 0]
    drain(stats, roll, recv_sem.at[STATS])
    top = jnp.max(stats[:, 0], axis=0)
    factor = jnp.exp(stats[:, 0] - top[None])
    total = jnp.sum(stats[:, 1] * factor, axis=0)
    delta = jnp.sum(stats[:, 2] * factor, axis=0) / total
    norm = jnp.exp(own_top - top) / total

    key_grad = jnp.zeros((keys, hd), F32)
    value_grad = jnp.zeros((keys, hd), F32)
    halves = []
    for h in range(HEADS):
        cols = pl.ds(h * hd, hd)
        prob = expo[h] * norm[h : h + 1]
        dscore = (prob * (dprob[h] - delta[h : h + 1])).astype(BF)
        halves.append(dscore)
        key_grad += contract(dscore, q_in[:, cols], ((1,), (0,)))
        value_grad += contract(prob.astype(BF), do_in[:, cols], ((1,), (0,)))
    both = jnp.concatenate(
        [(key_grad * scale).reshape(ctx, SHARE, hd), value_grad.reshape(ctx, SHARE, hd)], axis=1
    )
    dkv_to[...] = both.astype(BF)
    push(
        "ctx", c, ctx, lambda peer: dkv_to.at[peer], dkv_from.at[c], send_sem.at[DKV], recv_sem.at[DKV]
    )
    dkv_from[c] = dkv_to[c]

    query_parts = [contract(half, key, ((0,), (0,))) for half in halves]
    dq_to[...] = jnp.concatenate(query_parts, axis=0).astype(BF).reshape(roll, piece, hd)
    push(
        "roll", r, roll, lambda peer: dq_to.at[peer], dq_from.at[r], send_sem.at[DQ], recv_sem.at[DQ]
    )
    dq_from[r] = dq_to[r]

    drain(dkv_from, ctx, recv_sem.at[DKV])
    kvg[r] = jnp.sum(dkv_from[...].astype(F32), axis=0).astype(BF)
    push("roll", r, roll, lambda peer: kvg.at[r], kvg.at[r], send_sem.at[KVG], recv_sem.at[KVG])
    loads[6].wait()
    drain(kvg, roll, recv_sem.at[KVG])
    wide = kvg[...].astype(F32)
    kv_wide[0] = wide[:, :SHARE, :].reshape(rows, hd)
    kv_wide[1] = wide[:, SHARE:, :].reshape(rows, hd)
    key_grad = kv_wide[0].astype(BF)
    product = contract(x_in[...].reshape(ctx * OWN, rows), key_grad, ((1,), (0,)))
    wg_to[...] = product.astype(BF).reshape(ctx, OWN, hd)
    push("ctx", c, ctx, lambda peer: wg_to.at[peer], wg_from.at[c], send_sem.at[WG], recv_sem.at[WG])
    wg_from[c] = wg_to[c]

    kvg_stage[:, :hd] = key_grad
    kvg_stage[:, hd:] = kv_wide[1].astype(BF)
    outs = [pltpu.make_async_copy(kvg_stage, kvg_out, out_sem.at[0])]
    outs[0].start()

    drain(dq_from, roll, recv_sem.at[DQ])
    dq_all[r] = (jnp.sum(dq_from[...].astype(F32), axis=0) * scale).astype(BF)
    push(
        "roll", r, roll, lambda peer: dq_all.at[r], dq_all.at[r], send_sem.at[DQALL], recv_sem.at[DQALL]
    )

    for i in (7, 8, 9):
        loads[i].wait()
    drain(wg_from, ctx, recv_sem.at[WG])
    grad = jnp.sum(wg_from[...].astype(F32), axis=0)
    master = mw_in[...]
    new_first = BETA_ONE * m1_in[...] + (1.0 - BETA_ONE) * grad
    new_second = BETA_TWO * m2_in[...] + (1.0 - BETA_TWO) * grad * grad
    update = (
        new_first / CORRECT_ONE / (jnp.sqrt(new_second / CORRECT_TWO) + ADAM_EPS)
        + DECAY_RATE * master
    )
    new_master = master - LEARN_RATE * update
    rolled[r] = new_master.astype(BF)
    push("roll", r, roll, lambda peer: rolled.at[r], rolled.at[r], send_sem.at[ROLL], recv_sem.at[ROLL])
    mw_stage[...] = new_master
    m1_stage[...] = new_first
    m2_stage[...] = new_second
    for stage, out in ((mw_stage, mw_out), (m1_stage, m1_out), (m2_stage, m2_out)):
        outs.append(pltpu.make_async_copy(stage, out, out_sem.at[len(outs)]))
        outs[-1].start()

    drain(dq_all, roll, recv_sem.at[DQALL])
    flat = dq_all[...].reshape(HEADS * rows, hd)
    for h in range(HEADS):
        qg_stage[:, pl.ds(h * hd, hd)] = flat[h * rows : (h + 1) * rows]
    outs.append(pltpu.make_async_copy(qg_stage, qg_out, out_sem.at[len(outs)]))
    outs[-1].start()
    drain(rolled, roll, recv_sem.at[ROLL])
    outs.append(pltpu.make_async_copy(rolled, rw_out, out_sem.at[len(outs)]))
    outs[-1].start()

    for buf, count, which in (
        (kv, ctx, KV),
        (stats, roll, STATS),
        (dkv_to, ctx, DKV),
        (dq_to, roll, DQ),
        (dq_all, roll, DQALL),
        (kvg, roll, KVG),
        (wg_to, ctx, WG),
        (rolled, roll, ROLL),
    ):
        drain(buf, count, send_sem.at[which])
    for out in outs:
        out.wait()


def body(order, segments, layer_input, query, key, value, out_grad, master, first, second):
    ctx = lax.axis_size("ctx")
    roll = lax.axis_size("roll")
    rows, hd = key.shape
    width = query.shape[1]
    keys = ctx * SHARE
    piece = HEADS * SHARE
    shape = jax.ShapeDtypeStruct
    vmem = pltpu.VMEM
    anywhere = pl.BlockSpec(memory_space=pl.ANY)
    query_grad, key_value, new_master, new_first, new_second, rolled = pl.pallas_call(
        functools.partial(kernel, ctx, roll),
        out_shape=(
            shape((rows, width), BF),
            shape((rows, 2 * hd), BF),
            shape((OWN, hd), F32),
            shape((OWN, hd), F32),
            shape((OWN, hd), F32),
            shape((roll, OWN, hd), BF),
        ),
        in_specs=[pl.BlockSpec(memory_space=pltpu.HBM)] * 10,
        out_specs=[anywhere] * 6,
        scratch_shapes=[
            pltpu.SMEM((ctx,), jnp.int32),
            vmem((ctx, rows), jnp.int32),
            vmem((ctx, OWN, rows), BF),
            vmem((rows, width), BF),
            vmem((rows, hd), BF),
            vmem((rows, hd), BF),
            vmem((rows, width), BF),
            vmem((OWN, hd), F32),
            vmem((OWN, hd), F32),
            vmem((OWN, hd), F32),
            vmem((2, rows, hd), F32),
            vmem((keys, rows), F32),
            vmem((HEADS, keys, rows), F32),
            vmem((HEADS, keys, rows), F32),
            vmem((ctx, 2 * SHARE, hd), BF),
            vmem((roll, 3, 8, rows), F32),
            vmem((ctx, 2 * SHARE, hd), BF),
            vmem((ctx, 2 * SHARE, hd), BF),
            vmem((roll, piece, hd), BF),
            vmem((roll, piece, hd), BF),
            vmem((roll, piece, hd), BF),
            vmem((roll, 2 * SHARE, hd), BF),
            vmem((ctx, OWN, hd), BF),
            vmem((ctx, OWN, hd), BF),
            vmem((roll, OWN, hd), BF),
            vmem((rows, width), BF),
            vmem((rows, 2 * hd), BF),
            vmem((OWN, hd), F32),
            vmem((OWN, hd), F32),
            vmem((OWN, hd), F32),
            pltpu.SemaphoreType.DMA((10,)),
            pltpu.SemaphoreType.DMA((10,)),
            pltpu.SemaphoreType.DMA((10,)),
            pltpu.SemaphoreType.DMA((6,)),
        ],
        compiler_params=pltpu.CompilerParams(
            collective_id=0, has_side_effects=True, vmem_limit_bytes=56 * 1024 * 1024
        ),
    )(
        order,
        segments.reshape(ctx, rows),
        layer_input.reshape(ctx, roll, OWN, rows),
        query,
        key,
        value,
        out_grad,
        master,
        first,
        second,
    )
    return (
        query_grad,
        key_value,
        new_master,
        new_first,
        new_second,
        rolled.reshape(roll * OWN, hd),
    )


def solution(mesh):
    placed = (
        P(),
        P(),
        P(None, "ctx"),
        P("ctx", None),
        P("ctx", None),
        P("ctx", None),
        P("ctx", None),
        P(("ctx", "roll"), None),
        P(("ctx", "roll"), None),
        P(("ctx", "roll"), None),
    )
    return jax.shard_map(
        body,
        mesh=mesh,
        in_specs=placed,
        out_specs=(
            P("ctx", None),
            P("ctx", None),
            P(("ctx", "roll"), None),
            P(("ctx", "roll"), None),
            P(("ctx", "roll"), None),
            P("ctx", None),
        ),
        check_vma=False,
    )
```

time: 261 us -> 75.2 us (0.29)
  the two profiles are of different devices: /device:TPU:1 before, /device:TPU:57 now
where the time goes in v1:
time: 75.2 us; the launch traced here: 74.8 us
  Pallas kernels  65.7 us (87%)
  local copies, waits for them, and re-layouts  8.45 us (11%)
    pallas_call x1, Pallas kernels, body(): pl.pallas_call(functools.partial(kernel, ctx, roll), out_shape=(shape((ro...  65.7 us
    unnamed x6, local copies, waits for them, and re-layouts  8.45 us

profile of v1, /device:TPU:57, one launch (start us, length us, event | category | flops | bytes accessed | tf_op | source)
XLA Modules:
  0.0 74.8 jit_solution(11318354483496798713)
XLA Ops:
  0.6 65.7 %shard_map.145 = (bf16[128,768]{1,0:T(8,128)(2,1)}, bf16[128,256]{1,0:T(8,128)(2,1)}, f32[16,128]{1,0:T(8,128)}, f32[16,128]{1,0:T(8,128)}, f32[16,128]{1,0:T(8,128)}, /*index=5*/bf16[16,16,128]{2,1,0:T(8,128)(2,1)}) custom-call(s32[32]{0:T(128)} %order_hbm.1, s32[32,128]{1,0:T(8,128)} %bitcast.5, bf16[32,16,16,128]{3,2,1,0:T(8,128)(2,1)} %bitcast.3, ...), custom_call_target="tpu_custom_call" | custom-call | tf_op jit(solution)/shard_map/pallas_call | solution.py:319
  66.4 1.6 %copy.22 = bf16[128,768]{1,0:T(8,128)(2,1)} copy(bf16[128,768]{1,0:T(8,128)(2,1)} %get-tuple-element.24) | data formatting | bytes 393216
  68.0 1.5 %copy.23 = bf16[128,256]{1,0:T(8,128)(2,1)} copy(bf16[128,256]{1,0:T(8,128)(2,1)} %get-tuple-element.25) | data formatting | bytes 131072
  69.5 1.3 %copy.24 = f32[16,128]{1,0:T(8,128)} copy(f32[16,128]{1,0:T(8,128)} %get-tuple-element.26) | data formatting | bytes 16384
  70.8 1.3 %copy.25 = f32[16,128]{1,0:T(8,128)} copy(f32[16,128]{1,0:T(8,128)} %get-tuple-element.27) | data formatting | bytes 16384
  72.1 1.3 %copy.26 = f32[16,128]{1,0:T(8,128)} copy(f32[16,128]{1,0:T(8,128)} %get-tuple-element.28) | data formatting | bytes 16384
  73.4 1.5 %copy.27 = bf16[256,128]{1,0:T(8,128)(2,1)} copy(bf16[256,128]{1,0:T(8,128)(2,1)} %bitcast.4) | data formatting | bytes 131072

commit v2 on v1

v2 whole, which is shorter than its diff:
```python
import functools

import jax
import jax.numpy as jnp
from jax import lax
from jax.experimental import pallas as pl
from jax.experimental.pallas import tpu as pltpu
from jax.sharding import PartitionSpec as P

NEG_FILL = -1e30
BETA_ONE = 0.9
BETA_TWO = 0.95
ADAM_EPS = 1e-08
DECAY_RATE = 0.1
LEARN_RATE = 1e-06
CORRECT_ONE = 0.9999734386011124
CORRECT_TWO = 0.994079470779666

MESH = pl.DeviceIdType.MESH
RING = 8
RUN = 4
SHARE = 8
OWN = 16
HEADS = 6
BF = jnp.bfloat16
F32 = jnp.float32

(KV, STATE, STATS, DKV, DQ, DQALL, KVG, WG, ROLL, BACK) = range(10)


class Place:
    def __init__(self, ctx, roll):
        self.zs, self.xs = ctx // RUN, roll // (2 * (RING // RUN))
        self.c, self.r = lax.axis_index("ctx"), lax.axis_index("roll")
        self.z = lax.rem(self.c, self.zs)
        self.x = lax.div(self.r, 4)
        self.core = lax.rem(self.r, 2)
        self.y = lax.div(self.c, self.zs) + RUN * lax.rem(lax.div(self.r, 2), 2)

    def turn(self, dy):
        return lax.rem(self.y + (dy + RING), RING)

    def block(self, y, z):
        return lax.rem(y, RUN) * self.zs + z

    def part(self, y, x=None, core=None):
        x = self.x if x is None else x
        core = self.core if core is None else core
        return x * 4 + lax.div(y, RUN) * 2 + core

    def device(self, y, z, x=None, core=None):
        return {"ctx": self.block(y, z), "roll": self.part(y, x, core)}

    def around_z(self, dz):
        return lax.rem(self.z + dz, self.zs)

    def across(self, steps):
        ways = [(dy, dx, dk) for dy in steps for dx in range(self.xs) for dk in range(2)]
        ways.sort(key=lambda w: -(min(w[0] % RING, -w[0] % RING) + min(w[1], self.xs - w[1])))
        return [
            (way, self.turn(way[0]), lax.rem(self.x + way[1], self.xs), lax.rem(self.core + way[2], 2))
            for way in ways
        ]

    def window(self, steps):
        ways = [(dy, dz) for dy in steps for dz in range(self.zs)]
        return sorted(ways, key=lambda w: -(abs(w[0]) + min(w[1], self.zs - w[1])))


def send(src, dst, sems, which, device):
    pltpu.make_async_remote_copy(
        src_ref=src,
        dst_ref=dst,
        send_sem=sems[0].at[which],
        recv_sem=sems[1].at[which],
        device_id=device,
        device_id_type=MESH,
    ).start()


def drain(part, sem):
    pltpu.make_async_copy(part, part, sem).wait()


def contract(left, right, dims):
    return lax.dot_general(left, right, (dims, ((), ())), preferred_element_type=F32)


def kernel(
    ctx,
    roll,
    order_hbm,
    seg_hbm,
    x_hbm,
    q_hbm,
    k_hbm,
    v_hbm,
    do_hbm,
    mw_hbm,
    m1_hbm,
    m2_hbm,
    qg_out,
    kvg_out,
    mw_out,
    m1_out,
    m2_out,
    rw_out,
    order,
    seg,
    x_in,
    q_in,
    k_in,
    v_in,
    do_in,
    state_in,
    state,
    state_new,
    state_back,
    kv_wide,
    bias,
    expo,
    dprob,
    kv,
    kv_other,
    stats,
    dkv_to,
    dkv_from,
    dq_to,
    dq_from,
    dq_all,
    kvg,
    kvg_own,
    wg_to,
    wg_from,
    rolled,
    rolled_own,
    kvg_stage,
    load_sem,
    send_sem,
    recv_sem,
    out_sem,
):
    at = Place(ctx, roll)
    c, r = at.c, at.r
    sems = (send_sem, recv_sem)
    rows = k_in.shape[0]
    hd = k_in.shape[1]
    keys = ctx * SHARE
    scale = hd**-0.5
    piece = HEADS * SHARE
    zs = at.zs
    most = pl.ds(0, ctx - 1)
    others = pl.ds(0, roll - 1)

    class_home = [
        lax.rem(at.y + RING - lax.rem(at.y + RING - j, RUN), RING) for j in range(RUN)
    ]
    class_part = [at.part(home) for home in class_home]

    pairs = [(k_hbm, k_in), (v_hbm, v_in), (order_hbm, order), (seg_hbm, seg)]
    pairs += [(src, state_in.at[i]) for i, src in enumerate((mw_hbm, m1_hbm, m2_hbm))]
    pairs += [(q_hbm, q_in), (do_hbm, do_in)]
    pairs += [
        (x_hbm.at[pl.ds(j * zs, zs), class_part[j]], x_in.at[pl.ds(j * zs, zs)]) for j in range(RUN)
    ]
    loads = [
        pltpu.make_async_copy(src, dst, load_sem.at[i]) for i, (src, dst) in enumerate(pairs)
    ]
    for load in loads:
        load.start()

    barrier = pltpu.get_barrier_semaphore()
    greeted = 0

    def greet(device):
        pl.semaphore_signal(barrier, inc=1, device_id=device, device_id_type=MESH)

    for dy, dz in at.window((1, 0, -1, -2)):
        if (dy, dz) != (0, 0):
            greet(at.device(at.turn(dy), at.around_z(dz)))
            greeted += 1
    for way, y, x, core in at.across((2, -2, 0, 4)):
        if way not in ((0, 0, 0), (-2, 0, 0)):
            greet(at.device(y, at.z, x, core))
            greeted += 1

    loads[0].wait()
    loads[1].wait()
    kv_wide[0] = k_in[...].astype(F32)
    kv_wide[1] = v_in[...].astype(F32)

    def chunk(part):
        first = pl.multiple_of(part * SHARE, SHARE)
        both = [kv_wide[i, pl.ds(first, SHARE), :] for i in range(2)]
        return jnp.concatenate(both, axis=0).astype(BF)

    kv[c] = chunk(r)
    kv_other[...] = chunk(at.part(at.turn(4)))
    pl.semaphore_wait(barrier, greeted)
    for dy, dz in at.window((2, 1, 0, -1)):
        if (dy, dz) != (0, 0):
            src = kv_other if dy == -1 else kv.at[c]
            send(src, kv.at[c], sems, KV, at.device(at.turn(dy), at.around_z(dz)))
    for i in (4, 5, 6):
        loads[i].wait()
    send(state_in, state, sems, STATE, at.device(at.turn(2), at.z))

    loads[2].wait()
    loads[3].wait()
    ids = seg[...]
    q_seg = seg[pl.ds(c, 1), :]
    lane = lax.broadcasted_iota(jnp.int32, (1, rows), 1)
    q_pos = order[c] * rows + lane
    start = jnp.zeros((1, rows), F32)
    for rollout in range(3):
        total = jnp.sum(jnp.where(ids == rollout, 1.0, 0.0), axis=0, keepdims=True)
        total = jnp.sum(total, axis=1, keepdims=True)
        start = start + jnp.where(q_seg > rollout, total, 0.0)
    start = start.astype(jnp.int32)
    sub = lax.broadcasted_iota(jnp.int32, (SHARE, rows), 0)
    latest = q_pos - sub
    earliest = start - sub
    for block in range(ctx):
        base = order[block] * rows + class_part[block // zs] * SHARE
        seen = (latest >= base) & (earliest <= base)
        bias[pl.ds(block * SHARE, SHARE), :] = jnp.where(seen, 0.0, NEG_FILL)

    loads[7].wait()
    loads[8].wait()
    heads = [pl.ds(h * hd, hd) for h in range(HEADS)]
    lanes = [pl.ds(h * rows, rows) for h in range(HEADS)]
    q_rows = jnp.concatenate([q_in[:, cols] for cols in heads], axis=0)
    do_rows = jnp.concatenate([do_in[:, cols] for cols in heads], axis=0)
    drain(kv.at[most], recv_sem.at[KV])
    wide = kv[...].astype(F32)
    key = wide[:, :SHARE, :].reshape(keys, hd).astype(BF)
    value = wide[:, SHARE:, :].reshape(keys, hd).astype(BF)
    expo[...] = contract(key, q_rows, ((1,), (1,)))
    dprob[...] = contract(value, do_rows, ((1,), (1,)))
    for h in range(HEADS):
        scores = expo[:, lanes[h]] * scale + bias[...]
        top = jnp.max(scores, axis=0, keepdims=True)
        weights = jnp.exp(scores - top)
        expo[:, lanes[h]] = weights
        stats[r, 0, h : h + 1] = top
        stats[r, 1, h : h + 1] = jnp.sum(weights, axis=0, keepdims=True)
        stats[r, 2, h : h + 1] = jnp.sum(weights * dprob[:, lanes[h]], axis=0, keepdims=True)
    for i in range(3):
        stats[r, i, HEADS:] = jnp.zeros((8 - HEADS, rows), F32)
    for way, y, x, core in at.across((4, 0)):
        if way != (0, 0, 0):
            send(stats.at[r], stats.at[r], sems, STATS, at.device(y, at.z, x, core))
    own_top = stats[r, 0]
    drain(stats.at[others], recv_sem.at[STATS])
    top = jnp.max(stats[:, 0], axis=0)
    factor = jnp.exp(stats[:, 0] - top[None])
    total = jnp.sum(stats[:, 1] * factor, axis=0)
    delta = jnp.sum(stats[:, 2] * factor, axis=0) / total
    norm = jnp.exp(own_top - top) / total

    probs, dscores = [], []
    for h in range(HEADS):
        prob = expo[:, lanes[h]] * norm[h : h + 1]
        dscores.append((prob * (dprob[:, lanes[h]] - delta[h : h + 1])).astype(BF))
        probs.append(prob.astype(BF))
    dscore = jnp.concatenate(dscores, axis=1)
    key_grad = contract(dscore, q_rows, ((1,), (0,))) * scale
    value_grad = contract(jnp.concatenate(probs, axis=1), do_rows, ((1,), (0,)))
    both = jnp.concatenate(
        [key_grad.reshape(ctx, SHARE, hd), value_grad.reshape(ctx, SHARE, hd)], axis=1
    )
    dkv_to[...] = both.astype(BF)

    back = at.turn(-2)
    back_block = at.block(back, at.z)
    back_part = at.part(back)

    def scatter(to, arrived, which):
        for dy, dz in at.window((2, 1, 0, -1)):
            z = at.around_z(dz)
            if (dy, dz) != (0, 0):
                home = at.block(at.turn(dy - 2), z)
                send(to.at[home], arrived.at[c], sems, which, at.device(at.turn(dy), z))
        arrived[c] = to[back_block]

    scatter(dkv_to, dkv_from, DKV)

    dq_to[...] = contract(dscore, key, ((0,), (0,))).astype(BF)

    def dq_piece(part):
        return pl.ds(pl.multiple_of(part * piece, 16), piece)

    for way, y, x, core in at.across((4, 0)):
        if way != (0, 0, 0):
            src = dq_to.at[dq_piece(at.part(y, x, core))]
            send(src, dq_from.at[r], sems, DQ, at.device(y, at.z, x, core))
    dq_from[r] = dq_to[dq_piece(r)]

    drain(dkv_from.at[most], recv_sem.at[DKV])
    kvg_own[...] = jnp.sum(dkv_from[...].astype(F32), axis=0).astype(BF)

    def spread(own, arrived, which):
        for _, y, x, core in at.across((2, -2)):
            send(own, arrived.at[back_part], sems, which, at.device(y, at.z, x, core))

    spread(kvg_own, kvg, KVG)
    for load in loads[9:]:
        load.wait()
    drain(kvg, recv_sem.at[KVG])
    wide = kvg[...].astype(F32)
    kv_wide[0] = wide[:, :SHARE, :].reshape(rows, hd)
    kv_wide[1] = wide[:, SHARE:, :].reshape(rows, hd)
    key_grad = kv_wide[0].astype(BF)
    product = contract(x_in[...].reshape(ctx * OWN, rows), key_grad, ((1,), (0,)))
    wg_to[...] = product.astype(BF).reshape(ctx, OWN, hd)
    scatter(wg_to, wg_from, WG)

    kvg_stage[:, :hd] = key_grad
    kvg_stage[:, hd:] = kv_wide[1].astype(BF)
    outs = []

    def put(src, dst):
        outs.append(pltpu.make_async_copy(src, dst, out_sem.at[len(outs)]))
        outs[-1].start()

    put(kvg_stage, kvg_out)
    drain(dq_from.at[others], recv_sem.at[DQ])
    dq_all[dq_piece(r)] = (jnp.sum(dq_from[...].astype(F32), axis=0) * scale).astype(BF)
    for way, y, x, core in at.across((4, 0)):
        if way != (0, 0, 0):
            mine = dq_all.at[dq_piece(r)]
            send(mine, mine, sems, DQALL, at.device(y, at.z, x, core))

    drain(state, recv_sem.at[STATE])
    drain(wg_from.at[most], recv_sem.at[WG])
    grad = jnp.sum(wg_from[...].astype(F32), axis=0)
    master = state[0]
    new_first = BETA_ONE * state[1] + (1.0 - BETA_ONE) * grad
    new_second = BETA_TWO * state[2] + (1.0 - BETA_TWO) * grad * grad
    update = (
        new_first / CORRECT_ONE / (jnp.sqrt(new_second / CORRECT_TWO) + ADAM_EPS)
        + DECAY_RATE * master
    )
    new_master = master - LEARN_RATE * update
    rolled_own[...] = new_master.astype(BF)
    spread(rolled_own, rolled, ROLL)
    state_new[0] = new_master
    state_new[1] = new_first
    state_new[2] = new_second
    send(state_new, state_back, sems, BACK, at.device(back, at.z))

    dq_most = pl.ds(0, (roll - 1) * piece)
    drain(dq_all.at[dq_most], recv_sem.at[DQALL])
    for h in range(HEADS):
        put(dq_all.at[pl.ds(h * rows, rows)], qg_out.at[:, heads[h]])
    drain(kv.at[most], send_sem.at[KV])
    drain(state_in, send_sem.at[STATE])
    drain(stats.at[others], send_sem.at[STATS])
    drain(dkv_to.at[most], send_sem.at[DKV])
    drain(dq_to.at[dq_most], send_sem.at[DQ])
    drain(kvg, send_sem.at[KVG])
    drain(wg_to.at[most], send_sem.at[WG])
    drain(dq_all.at[dq_most], send_sem.at[DQALL])
    drain(state_back, recv_sem.at[BACK])
    for i, out in enumerate((mw_out, m1_out, m2_out)):
        put(state_back.at[i], out)
    drain(rolled, recv_sem.at[ROLL])
    put(rolled, rw_out)
    drain(rolled, send_sem.at[ROLL])
    drain(state_new, send_sem.at[BACK])
    for out in outs:
        out.wait()


def hand_over(*refs):
    *arrays, sem = refs
    half = len(arrays) // 2
    copies = [
        pltpu.make_async_copy(src, dst, sem.at[i])
        for i, (src, dst) in enumerate(zip(arrays[:half], arrays[half:]))
    ]
    for copy in copies:
        copy.start()
    for copy in copies:
        copy.wait()


def body(order, segments, layer_input, query, key, value, out_grad, master, first, second):
    ctx = lax.axis_size("ctx")
    roll = lax.axis_size("roll")
    rows, hd = key.shape
    width = query.shape[1]
    keys = ctx * SHARE
    piece = HEADS * SHARE
    shape = jax.ShapeDtypeStruct
    vmem = pltpu.VMEM
    anywhere = pl.BlockSpec(memory_space=pl.ANY)
    shapes = (
        shape((rows, width), BF),
        shape((rows, 2 * hd), BF),
        shape((OWN, hd), F32),
        shape((OWN, hd), F32),
        shape((OWN, hd), F32),
        shape((roll, OWN, hd), BF),
    )
    made = pl.pallas_call(
        functools.partial(kernel, ctx, roll),
        out_shape=shapes,
        in_specs=[anywhere] * 10,
        out_specs=[anywhere] * 6,
        scratch_shapes=[
            pltpu.SMEM((ctx,), jnp.int32),
            vmem((ctx, rows), jnp.int32),
            vmem((ctx, OWN, rows), BF),
            vmem((rows, width), BF),
            vmem((rows, hd), BF),
            vmem((rows, hd), BF),
            vmem((rows, width), BF),
            vmem((3, OWN, hd), F32),
            vmem((3, OWN, hd), F32),
            vmem((3, OWN, hd), F32),
            vmem((3, OWN, hd), F32),
            vmem((2, rows, hd), F32),
            vmem((keys, rows), F32),
            vmem((keys, HEADS * rows), F32),
            vmem((keys, HEADS * rows), F32),
            vmem((ctx, 2 * SHARE, hd), BF),
            vmem((2 * SHARE, hd), BF),
            vmem((roll, 3, 8, rows), F32),
            vmem((ctx, 2 * SHARE, hd), BF),
            vmem((ctx, 2 * SHARE, hd), BF),
            vmem((roll * piece, hd), BF),
            vmem((roll, piece, hd), BF),
            vmem((roll * piece, hd), BF),
            vmem((roll, 2 * SHARE, hd), BF),
            vmem((2 * SHARE, hd), BF),
            vmem((ctx, OWN, hd), BF),
            vmem((ctx, OWN, hd), BF),
            vmem((roll, OWN, hd), BF),
            vmem((OWN, hd), BF),
            vmem((rows, 2 * hd), BF),
            pltpu.SemaphoreType.DMA((13,)),
            pltpu.SemaphoreType.DMA((10,)),
            pltpu.SemaphoreType.DMA((10,)),
            pltpu.SemaphoreType.DMA((12,)),
        ],
        compiler_params=pltpu.CompilerParams(
            collective_id=0, has_side_effects=True, vmem_limit_bytes=56 * 1024 * 1024
        ),
    )(
        order,
        segments.reshape(ctx, rows),
        layer_input.reshape(ctx, roll, OWN, rows),
        query,
        key,
        value,
        out_grad,
        master,
        first,
        second,
    )
    query_grad, key_value, new_master, new_first, new_second, rolled = pl.pallas_call(
        hand_over,
        out_shape=shapes,
        in_specs=[anywhere] * 6,
        out_specs=[anywhere] * 6,
        scratch_shapes=[pltpu.SemaphoreType.DMA((6,))],
    )(*made)
    return (
        query_grad,
        key_value,
        new_master,
        new_first,
        new_second,
        rolled.reshape(roll * OWN, hd),
    )


def solution(mesh):
    placed = (
        P(),
        P(),
        P(None, "ctx"),
        P("ctx", None),
        P("ctx", None),
        P("ctx", None),
        P("ctx", None),
        P(("ctx", "roll"), None),
        P(("ctx", "roll"), None),
        P(("ctx", "roll"), None),
    )
    return jax.shard_map(
        body,
        mesh=mesh,
        in_specs=placed,
        out_specs=(
            P("ctx", None),
            P("ctx", None),
            P(("ctx", "roll"), None),
            P(("ctx", "roll"), None),
            P(("ctx", "roll"), None),
            P("ctx", None),
        ),
        check_vma=False,
    )
```

time: 75.2 us -> 72.5 us (0.964)
  the two profiles are of different devices: /device:TPU:57 before, /device:TPU:1 now
where the time goes in v2:
time: 72.5 us; the launch traced here: 72.4 us
  Pallas kernels  71.8 us (99%)
    pallas_call x1, Pallas kernels, body(): pl.pallas_call(functools.partial(kernel, ctx, roll), out_shape=shapes, in...  59.9 us
    pallas_call x1, Pallas kernels, body(): pl.pallas_call(hand_over, out_shape=shapes, in_specs=[anywhere] * 6, out_...  11.8 us

profile of v2, /device:TPU:1, one launch (start us, length us, event | category | flops | bytes accessed | tf_op | source)
XLA Modules:
  0.0 72.4 jit_solution(17599800590461327788)
XLA Ops:
  0.6 59.9 %shard_map.145 = (bf16[128,768]{1,0:T(8,128)(2,1)}, bf16[128,256]{1,0:T(8,128)(2,1)}, f32[16,128]{1,0:T(8,128)}, f32[16,128]{1,0:T(8,128)}, f32[16,128]{1,0:T(8,128)}, /*index=5*/bf16[16,16,128]{2,1,0:T(8,128)(2,1)}) custom-call(s32[32]{0:T(128)} %order_hbm.1, s32[32,128]{1,0:T(8,128)} %bitcast.4, bf16[32,16,16,128]{3,2,1,0:T(8,128)(2,1)} %bitcast.3, ...), custom_call_target="tpu_custom_call" | custom-call | tf_op jit(solution)/shard_map/pallas_call | solution.py:406
  60.6 11.8 %shard_map.146 = (bf16[128,768]{1,0:T(8,128)(2,1)}, bf16[128,256]{1,0:T(8,128)(2,1)}, f32[16,128]{1,0:T(8,128)}, f32[16,128]{1,0:T(8,128)}, f32[16,128]{1,0:T(8,128)}, /*index=5*/bf16[16,16,128]{2,1,0:T(8,128)(2,1)}) custom-call(bf16[128,768]{1,0:T(8,128)(2,1)} %get-tuple-element.18.refs_0_, bf16[128,256]{1,0:T(8,128)(2,1)} %get-tuple-element.19.refs_1_, ...), custom_call_target="tpu_custom_call" | custom-call | tf_op jit(solution)/shard_map/pallas_call | solution.py:462

commit v3 on v2

--- a/solution.py
+++ b/solution.py
@@ -115,24 +115,23 @@
     state_in,
     state,
     state_new,
-    state_back,
     kv_wide,
     bias,
     expo,
     dprob,
     kv,
     kv_other,
+    tops,
     stats,
     dkv_to,
     dkv_from,
     dq_to,
     dq_from,
-    dq_all,
+    dq_own,
     kvg,
     kvg_own,
     wg_to,
     wg_from,
-    rolled,
     rolled_own,
     kvg_stage,
     load_sem,
@@ -166,7 +165,7 @@
     loads = [
         pltpu.make_async_copy(src, dst, load_sem.at[i]) for i, (src, dst) in enumerate(pairs)
     ]
-    for load in loads:
+    for load in loads[:2]:
         load.start()
 
     barrier = pltpu.get_barrier_semaphore()
@@ -183,6 +182,9 @@
         if way not in ((0, 0, 0), (-2, 0, 0)):
             greet(at.device(y, at.z, x, core))
             greeted += 1
+
+    for load in loads[2:]:
+        load.start()
 
     loads[0].wait()
     loads[1].wait()
@@ -242,21 +244,24 @@
         top = jnp.max(scores, axis=0, keepdims=True)
         weights = jnp.exp(scores - top)
         expo[:, lanes[h]] = weights
-        stats[r, 0, h : h + 1] = top
-        stats[r, 1, h : h + 1] = jnp.sum(weights, axis=0, keepdims=True)
-        stats[r, 2, h : h + 1] = jnp.sum(weights * dprob[:, lanes[h]], axis=0, keepdims=True)
-    for i in range(3):
+        total = jnp.sum(weights, axis=0, keepdims=True)
+        tops[h : h + 1] = top
+        stats[r, 0, h : h + 1] = top + jnp.log(total)
+        stats[r, 1, h : h + 1] = (
+            jnp.sum(weights * dprob[:, lanes[h]], axis=0, keepdims=True) / total
+        )
+    tops[HEADS:] = jnp.zeros((8 - HEADS, rows), F32)
+    for i in range(2):
         stats[r, i, HEADS:] = jnp.zeros((8 - HEADS, rows), F32)
     for way, y, x, core in at.across((4, 0)):
         if way != (0, 0, 0):
             send(stats.at[r], stats.at[r], sems, STATS, at.device(y, at.z, x, core))
-    own_top = stats[r, 0]
     drain(stats.at[others], recv_sem.at[STATS])
     top = jnp.max(stats[:, 0], axis=0)
     factor = jnp.exp(stats[:, 0] - top[None])
-    total = jnp.sum(stats[:, 1] * factor, axis=0)
-    delta = jnp.sum(stats[:, 2] * factor, axis=0) / total
-    norm = jnp.exp(own_top - top) / total
+    total = jnp.sum(factor, axis=0)
+    delta = jnp.sum(stats[:, 1] * factor, axis=0) / total
+    norm = jnp.exp(tops[...] - top) / total
 
     probs, dscores = [], []
     for h in range(HEADS):
@@ -285,6 +290,15 @@
 
     scatter(dkv_to, dkv_from, DKV)
 
+    drain(dkv_from.at[most], recv_sem.at[DKV])
+    kvg_own[...] = jnp.sum(dkv_from[...].astype(F32), axis=0).astype(BF)
+
+    def spread(own, arrived, which):
+        for _, y, x, core in at.across((2, -2)):
+            send(own, arrived.at[back_part], sems, which, at.device(y, at.z, x, core))
+
+    spread(kvg_own, kvg, KVG)
+
     dq_to[...] = contract(dscore, key, ((0,), (0,))).astype(BF)
 
     def dq_piece(part):
@@ -295,15 +309,6 @@
             src = dq_to.at[dq_piece(at.part(y, x, core))]
             send(src, dq_from.at[r], sems, DQ, at.device(y, at.z, x, core))
     dq_from[r] = dq_to[dq_piece(r)]
-
-    drain(dkv_from.at[most], recv_sem.at[DKV])
-    kvg_own[...] = jnp.sum(dkv_from[...].astype(F32), axis=0).astype(BF)
-
-    def spread(own, arrived, which):
-        for _, y, x, core in at.across((2, -2)):
-            send(own, arrived.at[back_part], sems, which, at.device(y, at.z, x, core))
-
-    spread(kvg_own, kvg, KVG)
     for load in loads[9:]:
         load.wait()
     drain(kvg, recv_sem.at[KVG])
@@ -325,11 +330,12 @@
 
     put(kvg_stage, kvg_out)
     drain(dq_from.at[others], recv_sem.at[DQ])
-    dq_all[dq_piece(r)] = (jnp.sum(dq_from[...].astype(F32), axis=0) * scale).astype(BF)
+    dq_own[...] = (jnp.sum(dq_from[...].astype(F32), axis=0) * scale).astype(BF)
+    mine = qg_out.at[dq_piece(r)]
     for way, y, x, core in at.across((4, 0)):
         if way != (0, 0, 0):
-            mine = dq_all.at[dq_piece(r)]
-            send(mine, mine, sems, DQALL, at.device(y, at.z, x, core))
+            send(dq_own, mine, sems, DQALL, at.device(y, at.z, x, core))
+    put(dq_own, mine)
 
     drain(state, recv_sem.at[STATE])
     drain(wg_from.at[most], recv_sem.at[WG])
@@ -343,16 +349,14 @@
     )
     new_master = master - LEARN_RATE * update
     rolled_own[...] = new_master.astype(BF)
-    spread(rolled_own, rolled, ROLL)
+    spread(rolled_own, rw_out, ROLL)
     state_new[0] = new_master
     state_new[1] = new_first
     state_new[2] = new_second
-    send(state_new, state_back, sems, BACK, at.device(back, at.z))
+    for i, out in enumerate((mw_out, m1_out, m2_out)):
+        send(state_new.at[i], out, sems, BACK, at.device(back, at.z))
 
     dq_most = pl.ds(0, (roll - 1) * piece)
-    drain(dq_all.at[dq_most], recv_sem.at[DQALL])
-    for h in range(HEADS):
-        put(dq_all.at[pl.ds(h * rows, rows)], qg_out.at[:, heads[h]])
     drain(kv.at[most], send_sem.at[KV])
     drain(state_in, send_sem.at[STATE])
     drain(stats.at[others], send_sem.at[STATS])
@@ -360,29 +364,40 @@
     drain(dq_to.at[dq_most], send_sem.at[DQ])
     drain(kvg, send_sem.at[KVG])
     drain(wg_to.at[most], send_sem.at[WG])
-    drain(dq_all.at[dq_most], send_sem.at[DQALL])
-    drain(state_back, recv_sem.at[BACK])
-    for i, out in enumerate((mw_out, m1_out, m2_out)):
-        put(state_back.at[i], out)
-    drain(rolled, recv_sem.at[ROLL])
-    put(rolled, rw_out)
-    drain(rolled, send_sem.at[ROLL])
+    drain(dq_to.at[dq_most], send_sem.at[DQALL])
+    drain(kvg, send_sem.at[ROLL])
     drain(state_new, send_sem.at[BACK])
+    drain(state_new, recv_sem.at[BACK])
+    drain(dq_to.at[dq_most], recv_sem.at[DQALL])
+    drain(kvg, recv_sem.at[ROLL])
     for out in outs:
         out.wait()
 
 
 def hand_over(*refs):
-    *arrays, sem = refs
-    half = len(arrays) // 2
-    copies = [
-        pltpu.make_async_copy(src, dst, sem.at[i])
-        for i, (src, dst) in enumerate(zip(arrays[:half], arrays[half:]))
+    sources, places, held, sem = refs[:6], refs[6:12], refs[12:18], refs[18]
+    rows, hd = places[0].shape[0], sources[0].shape[1]
+    pairs = [(i, src, held[i]) for i, src in enumerate(sources)][1:]
+    pairs += [
+        (0, sources[0].at[pl.ds(h * rows, rows)], held[0].at[:, pl.ds(h * hd, hd)])
+        for h in range(HEADS)
     ]
-    for copy in copies:
-        copy.start()
-    for copy in copies:
-        copy.wait()
+    fetches = [
+        (i, pltpu.make_async_copy(src, dst, sem.at[0, n])) for n, (i, src, dst) in enumerate(pairs)
+    ]
+    writes = [
+        pltpu.make_async_copy(src, dst, sem.at[1, i])
+        for i, (src, dst) in enumerate(zip(held, places))
+    ]
+    for _, fetch in fetches:
+        fetch.start()
+    for i, fetch in fetches:
+        fetch.wait()
+        if i > 0:
+            writes[i].start()
+    writes[0].start()
+    for write in writes:
+        write.wait()
 
 
 def body(order, segments, layer_input, query, key, value, out_grad, master, first, second):
@@ -405,7 +420,7 @@
     )
     made = pl.pallas_call(
         functools.partial(kernel, ctx, roll),
-        out_shape=shapes,
+        out_shape=(shape((HEADS * rows, hd), BF), *shapes[1:]),
         in_specs=[anywhere] * 10,
         out_specs=[anywhere] * 6,
         scratch_shapes=[
@@ -419,24 +434,23 @@
             vmem((3, OWN, hd), F32),
             vmem((3, OWN, hd), F32),
             vmem((3, OWN, hd), F32),
-            vmem((3, OWN, hd), F32),
             vmem((2, rows, hd), F32),
             vmem((keys, rows), F32),
             vmem((keys, HEADS * rows), F32),
             vmem((keys, HEADS * rows), F32),
             vmem((ctx, 2 * SHARE, hd), BF),
             vmem((2 * SHARE, hd), BF),
-            vmem((roll, 3, 8, rows), F32),
+            vmem((8, rows), F32),
+            vmem((roll, 2, 8, rows), F32),
             vmem((ctx, 2 * SHARE, hd), BF),
             vmem((ctx, 2 * SHARE, hd), BF),
             vmem((roll * piece, hd), BF),
             vmem((roll, piece, hd), BF),
-            vmem((roll * piece, hd), BF),
+            vmem((piece, hd), BF),
             vmem((roll, 2 * SHARE, hd), BF),
             vmem((2 * SHARE, hd), BF),
             vmem((ctx, OWN, hd), BF),
             vmem((ctx, OWN, hd), BF),
-            vmem((roll, OWN, hd), BF),
             vmem((OWN, hd), BF),
             vmem((rows, 2 * hd), BF),
             pltpu.SemaphoreType.DMA((13,)),
@@ -464,7 +478,7 @@
         out_shape=shapes,
         in_specs=[anywhere] * 6,
         out_specs=[anywhere] * 6,
-        scratch_shapes=[pltpu.SemaphoreType.DMA((6,))],
+        scratch_shapes=[*(vmem(s.shape, s.dtype) for s in shapes), pltpu.SemaphoreType.DMA((2, 11))],
     )(*made)
     return (
         query_grad,

time: 72.5 us -> 59.2 us (0.82)
  Pallas kernels: 71.8 us -> 58.3 us
    pallas_call x1, Pallas kernels: 11.8 us -> 1.83 us  [body(): pl.pallas_call(hand_over, out_shape=shapes, in_specs=[anywhere] * 6, out_...]
    pallas_call x1, Pallas kernels: 59.9 us -> 56.5 us  [body(): pl.pallas_call(functools.partial(kernel, ctx, roll), out_shape=(shape((HE...]
where the time goes in v3:
time: 59.2 us; the launch traced here: 58.9 us
  Pallas kernels  58.3 us (98%)
  between operations  0.64 us (1%)
    pallas_call x1, Pallas kernels, body(): pl.pallas_call(functools.partial(kernel, ctx, roll), out_shape=(shape((HE...  56.5 us
    pallas_call x1, Pallas kernels, body(): pl.pallas_call(hand_over, out_shape=shapes, in_specs=[anywhere] * 6, out_...  1.83 us

profile of v3, /device:TPU:1, one launch (start us, length us, event | category | flops | bytes accessed | tf_op | source)
XLA Modules:
  0.0 58.9 jit_solution(9271791765169260485)
XLA Ops:
  0.6 56.5 %shard_map.145 = (bf16[768,128]{1,0:T(8,128)(2,1)}, bf16[128,256]{1,0:T(8,128)(2,1)}, f32[16,128]{1,0:T(8,128)}, f32[16,128]{1,0:T(8,128)}, f32[16,128]{1,0:T(8,128)}, /*index=5*/bf16[16,16,128]{2,1,0:T(8,128)(2,1)}) custom-call(s32[32]{0:T(128)} %order_hbm.1, s32[32,128]{1,0:T(8,128)} %bitcast.4, bf16[32,16,16,128]{3,2,1,0:T(8,128)(2,1)} %bitcast.3, ...), custom_call_target="tpu_custom_call" | custom-call | tf_op jit(solution)/shard_map/pallas_call | solution.py:421
  57.1 1.8 %shard_map.146 = (bf16[128,768]{1,0:T(8,128)(2,1)}, bf16[128,256]{1,0:T(8,128)(2,1)}, f32[16,128]{1,0:T(8,128)}, f32[16,128]{1,0:T(8,128)}, f32[16,128]{1,0:T(8,128)}, /*index=5*/bf16[16,16,128]{2,1,0:T(8,128)(2,1)}) custom-call(bf16[768,128]{1,0:T(8,128)(2,1)} %get-tuple-element.18.refs_0_, bf16[128,256]{1,0:T(8,128)(2,1)} %get-tuple-element.19.refs_1_, ...), custom_call_target="tpu_custom_call" | custom-call | tf_op jit(solution)/shard_map/pallas_call | solution.py:476

commit v4 on v3

--- a/solution.py
+++ b/solution.py
@@ -25,7 +25,7 @@
 BF = jnp.bfloat16
 F32 = jnp.float32
 
-(KV, STATE, STATS, DKV, DQ, DQALL, KVG, WG, ROLL, BACK) = range(10)
+(KV, STATE, STATS, DKV, PAIR, DQ, DQALL, GIVE, KVG, WG, ROLL, BACK) = range(12)
 
 
 class Place:
@@ -126,8 +126,10 @@
     dkv_to,
     dkv_from,
     dq_to,
+    dq_near,
+    dq_half,
     dq_from,
-    dq_own,
+    dq_side,
     kvg,
     kvg_own,
     wg_to,
@@ -300,15 +302,27 @@
     spread(kvg_own, kvg, KVG)
 
     dq_to[...] = contract(dscore, key, ((0,), (0,))).astype(BF)
-
-    def dq_piece(part):
-        return pl.ds(pl.multiple_of(part * piece, 16), piece)
-
-    for way, y, x, core in at.across((4, 0)):
-        if way != (0, 0, 0):
-            src = dq_to.at[dq_piece(at.part(y, x, core))]
-            send(src, dq_from.at[r], sems, DQ, at.device(y, at.z, x, core))
-    dq_from[r] = dq_to[dq_piece(r)]
+    sibling = at.device(at.y, at.z, at.x, 1 - at.core)
+    side = dq_half.shape[0]
+
+    def half(core):
+        return pl.ds(pl.multiple_of(core * side, 16), side)
+
+    def slot(y, x):
+        return x * 2 + lax.div(y, RUN)
+
+    def dq_piece(number):
+        return pl.ds(pl.multiple_of(number * piece, 16), piece)
+
+    mine = slot(at.y, at.x)
+    chips = [(y, x) for way, y, x, _ in at.across((4, 0)) if way[2] == 0 and way != (0, 0, 0)]
+    send(dq_to.at[half(1 - at.core)], dq_near, sems, PAIR, sibling)
+    drain(dq_near, recv_sem.at[PAIR])
+    dq_half[...] = (dq_to[half(at.core)].astype(F32) + dq_near[...].astype(F32)).astype(BF)
+    for y, x in chips:
+        send(dq_half.at[dq_piece(slot(y, x))], dq_from.at[mine], sems, DQ, at.device(y, at.z, x))
+    dq_from[mine] = dq_half[dq_piece(mine)]
+
     for load in loads[9:]:
         load.wait()
     drain(kvg, recv_sem.at[KVG])
@@ -329,13 +343,11 @@
         outs[-1].start()
 
     put(kvg_stage, kvg_out)
-    drain(dq_from.at[others], recv_sem.at[DQ])
-    dq_own[...] = (jnp.sum(dq_from[...].astype(F32), axis=0) * scale).astype(BF)
-    mine = qg_out.at[dq_piece(r)]
-    for way, y, x, core in at.across((4, 0)):
-        if way != (0, 0, 0):
-            send(dq_own, mine, sems, DQALL, at.device(y, at.z, x, core))
-    put(dq_own, mine)
+    drain(dq_from.at[pl.ds(0, len(chips))], recv_sem.at[DQ])
+    dq_side[dq_piece(mine)] = (jnp.sum(dq_from[...].astype(F32), axis=0) * scale).astype(BF)
+    summed = dq_side.at[dq_piece(mine)]
+    for y, x in chips:
+        send(summed, summed, sems, DQALL, at.device(y, at.z, x))
 
     drain(state, recv_sem.at[STATE])
     drain(wg_from.at[most], recv_sem.at[WG])
@@ -356,19 +368,24 @@
     for i, out in enumerate((mw_out, m1_out, m2_out)):
         send(state_new.at[i], out, sems, BACK, at.device(back, at.z))
 
-    dq_most = pl.ds(0, (roll - 1) * piece)
+    dq_most = pl.ds(0, len(chips) * piece)
+    drain(dq_side.at[dq_most], recv_sem.at[DQALL])
+    send(dq_side, qg_out.at[half(at.core)], sems, GIVE, sibling)
+    put(dq_side, qg_out.at[half(at.core)])
     drain(kv.at[most], send_sem.at[KV])
     drain(state_in, send_sem.at[STATE])
     drain(stats.at[others], send_sem.at[STATS])
     drain(dkv_to.at[most], send_sem.at[DKV])
-    drain(dq_to.at[dq_most], send_sem.at[DQ])
+    drain(dq_near, send_sem.at[PAIR])
+    drain(dq_side.at[dq_most], send_sem.at[DQ])
     drain(kvg, send_sem.at[KVG])
     drain(wg_to.at[most], send_sem.at[WG])
-    drain(dq_to.at[dq_most], send_sem.at[DQALL])
+    drain(dq_side.at[dq_most], send_sem.at[DQALL])
+    drain(dq_side, send_sem.at[GIVE])
     drain(kvg, send_sem.at[ROLL])
     drain(state_new, send_sem.at[BACK])
     drain(state_new, recv_sem.at[BACK])
-    drain(dq_to.at[dq_most], recv_sem.at[DQALL])
+    drain(dq_side, recv_sem.at[GIVE])
     drain(kvg, recv_sem.at[ROLL])
     for out in outs:
         out.wait()
@@ -445,8 +462,10 @@
             vmem((ctx, 2 * SHARE, hd), BF),
             vmem((ctx, 2 * SHARE, hd), BF),
             vmem((roll * piece, hd), BF),
-            vmem((roll, piece, hd), BF),
-            vmem((piece, hd), BF),
+            vmem((roll // 2 * piece, hd), BF),
+            vmem((roll // 2 * piece, hd), BF),
+            vmem((roll // 2, piece, hd), BF),
+            vmem((roll // 2 * piece, hd), BF),
             vmem((roll, 2 * SHARE, hd), BF),
             vmem((2 * SHARE, hd), BF),
             vmem((ctx, OWN, hd), BF),
@@ -454,8 +473,8 @@
             vmem((OWN, hd), BF),
             vmem((rows, 2 * hd), BF),
             pltpu.SemaphoreType.DMA((13,)),
-            pltpu.SemaphoreType.DMA((10,)),
-            pltpu.SemaphoreType.DMA((10,)),
+            pltpu.SemaphoreType.DMA((12,)),
+            pltpu.SemaphoreType.DMA((12,)),
             pltpu.SemaphoreType.DMA((12,)),
         ],
         compiler_params=pltpu.CompilerParams(

time: 59.2 us -> 55.8 us (0.943)
  Pallas kernels: 58.3 us -> 54.9 us
    pallas_call x1, Pallas kernels: 56.5 us -> 53.1 us  [body(): pl.pallas_call(functools.partial(kernel, ctx, roll), out_shape=(shape((HE...]
where the time goes in v4:
time: 55.8 us; the launch traced here: 55.6 us
  Pallas kernels  54.9 us (98%)
  between operations  0.64 us (1%)
    pallas_call x1, Pallas kernels, body(): pl.pallas_call(functools.partial(kernel, ctx, roll), out_shape=(shape((HE...  53.1 us
    pallas_call x1, Pallas kernels, body(): pl.pallas_call(hand_over, out_shape=shapes, in_specs=[anywhere] * 6, out_...  1.83 us

profile of v4, /device:TPU:1, one launch (start us, length us, event | category | flops | bytes accessed | tf_op | source)
XLA Modules:
  0.0 55.6 jit_solution(8029058445249168006)
XLA Ops:
  0.6 53.1 %shard_map.145 = (bf16[768,128]{1,0:T(8,128)(2,1)}, bf16[128,256]{1,0:T(8,128)(2,1)}, f32[16,128]{1,0:T(8,128)}, f32[16,128]{1,0:T(8,128)}, f32[16,128]{1,0:T(8,128)}, /*index=5*/bf16[16,16,128]{2,1,0:T(8,128)(2,1)}) custom-call(s32[32]{0:T(128)} %order_hbm.1, s32[32,128]{1,0:T(8,128)} %bitcast.4, bf16[32,16,16,128]{3,2,1,0:T(8,128)(2,1)} %bitcast.3, ...), custom_call_target="tpu_custom_call" | custom-call | tf_op jit(solution)/shard_map/pallas_call | solution.py:438
  53.7 1.8 %shard_map.146 = (bf16[128,768]{1,0:T(8,128)(2,1)}, bf16[128,256]{1,0:T(8,128)(2,1)}, f32[16,128]{1,0:T(8,128)}, f32[16,128]{1,0:T(8,128)}, f32[16,128]{1,0:T(8,128)}, /*index=5*/bf16[16,16,128]{2,1,0:T(8,128)(2,1)}) custom-call(bf16[768,128]{1,0:T(8,128)(2,1)} %get-tuple-element.18.refs_0_, bf16[128,256]{1,0:T(8,128)(2,1)} %get-tuple-element.19.refs_1_, ...), custom_call_target="tpu_custom_call" | custom-call | tf_op jit(solution)/shard_map/pallas_call | solution.py:495

commit v5 on v4

--- a/solution.py
+++ b/solution.py
@@ -80,6 +80,17 @@
 
 def drain(part, sem):
     pltpu.make_async_copy(part, part, sem).wait()
+
+
+def stepped(state, grad):
+    master = state[0]
+    new_first = BETA_ONE * state[1] + (1.0 - BETA_ONE) * grad
+    new_second = BETA_TWO * state[2] + (1.0 - BETA_TWO) * grad * grad
+    update = (
+        new_first / CORRECT_ONE / (jnp.sqrt(new_second / CORRECT_TWO) + ADAM_EPS)
+        + DECAY_RATE * master
+    )
+    return master - LEARN_RATE * update, new_first, new_second
 
 
 def contract(left, right, dims):
@@ -115,6 +126,8 @@
     state_in,
     state,
     state_new,
+    grad_own,
+    grad_back,
     kv_wide,
     bias,
     expo,
@@ -153,6 +166,13 @@
     most = pl.ds(0, ctx - 1)
     others = pl.ds(0, roll - 1)
 
+    ways = at.window((2, 1, 0, -1))
+    at_way = {way: n for n, way in enumerate(ways)}
+    homes = [(at.turn(dy - 2), at.around_z(dz)) for dy, dz in ways]
+    blocks = [at.block(y, z) for y, z in homes]
+    own_slot = at_way[2, 0]
+    last = len(ways) - 1
+
     class_home = [
         lax.rem(at.y + RING - lax.rem(at.y + RING - j, RUN), RING) for j in range(RUN)
     ]
@@ -185,9 +205,6 @@
             greet(at.device(y, at.z, x, core))
             greeted += 1
 
-    for load in loads[2:]:
-        load.start()
-
     loads[0].wait()
     loads[1].wait()
     kv_wide[0] = k_in[...].astype(F32)
@@ -198,13 +215,16 @@
         both = [kv_wide[i, pl.ds(first, SHARE), :] for i in range(2)]
         return jnp.concatenate(both, axis=0).astype(BF)
 
-    kv[c] = chunk(r)
+    kv[own_slot] = chunk(r)
     kv_other[...] = chunk(at.part(at.turn(4)))
     pl.semaphore_wait(barrier, greeted)
-    for dy, dz in at.window((2, 1, 0, -1)):
+    for dy, dz in ways:
         if (dy, dz) != (0, 0):
-            src = kv_other if dy == -1 else kv.at[c]
-            send(src, kv.at[c], sems, KV, at.device(at.turn(dy), at.around_z(dz)))
+            src = kv_other if dy == -1 else kv.at[own_slot]
+            there = at_way[-1 if dy == -1 else 2 - dy, -dz % zs]
+            send(src, kv.at[there], sems, KV, at.device(at.turn(dy), at.around_z(dz)))
+    for load in loads[2:]:
+        load.start()
     for i in (4, 5, 6):
         loads[i].wait()
     send(state_in, state, sems, STATE, at.device(at.turn(2), at.z))
@@ -224,10 +244,10 @@
     sub = lax.broadcasted_iota(jnp.int32, (SHARE, rows), 0)
     latest = q_pos - sub
     earliest = start - sub
-    for block in range(ctx):
-        base = order[block] * rows + class_part[block // zs] * SHARE
+    for n in range(ctx):
+        base = order[blocks[n]] * rows + at.part(homes[n][0]) * SHARE
         seen = (latest >= base) & (earliest <= base)
-        bias[pl.ds(block * SHARE, SHARE), :] = jnp.where(seen, 0.0, NEG_FILL)
+        bias[pl.ds(n * SHARE, SHARE), :] = jnp.where(seen, 0.0, NEG_FILL)
 
     loads[7].wait()
     loads[8].wait()
@@ -265,32 +285,34 @@
     delta = jnp.sum(stats[:, 1] * factor, axis=0) / total
     norm = jnp.exp(tops[...] - top) / total
 
-    probs, dscores = [], []
-    for h in range(HEADS):
-        prob = expo[:, lanes[h]] * norm[h : h + 1]
-        dscores.append((prob * (dprob[:, lanes[h]] - delta[h : h + 1])).astype(BF))
-        probs.append(prob.astype(BF))
-    dscore = jnp.concatenate(dscores, axis=1)
-    key_grad = contract(dscore, q_rows, ((1,), (0,))) * scale
-    value_grad = contract(jnp.concatenate(probs, axis=1), do_rows, ((1,), (0,)))
-    both = jnp.concatenate(
-        [key_grad.reshape(ctx, SHARE, hd), value_grad.reshape(ctx, SHARE, hd)], axis=1
-    )
-    dkv_to[...] = both.astype(BF)
-
     back = at.turn(-2)
     back_block = at.block(back, at.z)
     back_part = at.part(back)
-
-    def scatter(to, arrived, which):
-        for dy, dz in at.window((2, 1, 0, -1)):
-            z = at.around_z(dz)
-            if (dy, dz) != (0, 0):
-                home = at.block(at.turn(dy - 2), z)
-                send(to.at[home], arrived.at[c], sems, which, at.device(at.turn(dy), z))
-        arrived[c] = to[back_block]
-
-    scatter(dkv_to, dkv_from, DKV)
+    halves = [range(0, ctx // 2), range(ctx // 2, ctx)]
+
+    def scatter(part, to, arrived, which):
+        for n in part:
+            if n < last:
+                dy, dz = ways[n]
+                device = at.device(at.turn(dy), at.around_z(dz))
+                send(to.at[n], arrived.at[n], sems, which, device)
+
+    dscores = []
+    for part in halves:
+        span = pl.ds(part[0] * SHARE, keys // 2)
+        slots = pl.ds(part[0], ctx // 2)
+        probs, scored = [], []
+        for h in range(HEADS):
+            prob = expo[span, lanes[h]] * norm[h : h + 1]
+            scored.append((prob * (dprob[span, lanes[h]] - delta[h : h + 1])).astype(BF))
+            probs.append(prob.astype(BF))
+        dscores.append(jnp.concatenate(scored, axis=1))
+        key_grad = contract(dscores[-1], q_rows, ((1,), (0,))) * scale
+        value_grad = contract(jnp.concatenate(probs, axis=1), do_rows, ((1,), (0,)))
+        both = [g.reshape(ctx // 2, SHARE, hd) for g in (key_grad, value_grad)]
+        dkv_to[slots] = jnp.concatenate(both, axis=1).astype(BF)
+        scatter(part, dkv_to, dkv_from, DKV)
+    dkv_from[last] = dkv_to[last]
 
     drain(dkv_from.at[most], recv_sem.at[DKV])
     kvg_own[...] = jnp.sum(dkv_from[...].astype(F32), axis=0).astype(BF)
@@ -301,6 +323,7 @@
 
     spread(kvg_own, kvg, KVG)
 
+    dscore = jnp.concatenate(dscores, axis=0)
     dq_to[...] = contract(dscore, key, ((0,), (0,))).astype(BF)
     sibling = at.device(at.y, at.z, at.x, 1 - at.core)
     side = dq_half.shape[0]
@@ -330,9 +353,12 @@
     kv_wide[0] = wide[:, :SHARE, :].reshape(rows, hd)
     kv_wide[1] = wide[:, SHARE:, :].reshape(rows, hd)
     key_grad = kv_wide[0].astype(BF)
-    product = contract(x_in[...].reshape(ctx * OWN, rows), key_grad, ((1,), (0,)))
-    wg_to[...] = product.astype(BF).reshape(ctx, OWN, hd)
-    scatter(wg_to, wg_from, WG)
+    for part in halves:
+        taken = jnp.concatenate([x_in[blocks[n]] for n in part], axis=0)
+        product = contract(taken, key_grad, ((1,), (0,)))
+        wg_to[pl.ds(part[0], ctx // 2)] = product.astype(BF).reshape(ctx // 2, OWN, hd)
+        scatter(part, wg_to, wg_from, WG)
+    wg_from[last] = wg_to[last]
 
     kvg_stage[:, :hd] = key_grad
     kvg_stage[:, hd:] = kv_wide[1].astype(BF)
@@ -351,22 +377,17 @@
 
     drain(state, recv_sem.at[STATE])
     drain(wg_from.at[most], recv_sem.at[WG])
-    grad = jnp.sum(wg_from[...].astype(F32), axis=0)
-    master = state[0]
-    new_first = BETA_ONE * state[1] + (1.0 - BETA_ONE) * grad
-    new_second = BETA_TWO * state[2] + (1.0 - BETA_TWO) * grad * grad
-    update = (
-        new_first / CORRECT_ONE / (jnp.sqrt(new_second / CORRECT_TWO) + ADAM_EPS)
-        + DECAY_RATE * master
-    )
-    new_master = master - LEARN_RATE * update
-    rolled_own[...] = new_master.astype(BF)
+    grad_own[...] = jnp.sum(wg_from[...].astype(F32), axis=0)
+    send(grad_own, grad_back, sems, BACK, at.device(back, at.z))
+    rolled_own[...] = stepped(state, grad_own[...])[0].astype(BF)
     spread(rolled_own, rw_out, ROLL)
-    state_new[0] = new_master
-    state_new[1] = new_first
-    state_new[2] = new_second
-    for i, out in enumerate((mw_out, m1_out, m2_out)):
-        send(state_new.at[i], out, sems, BACK, at.device(back, at.z))
+
+    drain(grad_back, recv_sem.at[BACK])
+    for i, (new, out) in enumerate(
+        zip(stepped(state_in, grad_back[...]), (mw_out, m1_out, m2_out))
+    ):
+        state_new[i] = new
+        put(state_new.at[i], out)
 
     dq_most = pl.ds(0, len(chips) * piece)
     drain(dq_side.at[dq_most], recv_sem.at[DQALL])
@@ -383,8 +404,7 @@
     drain(dq_side.at[dq_most], send_sem.at[DQALL])
     drain(dq_side, send_sem.at[GIVE])
     drain(kvg, send_sem.at[ROLL])
-    drain(state_new, send_sem.at[BACK])
-    drain(state_new, recv_sem.at[BACK])
+    drain(grad_own, send_sem.at[BACK])
     drain(dq_side, recv_sem.at[GIVE])
     drain(kvg, recv_sem.at[ROLL])
     for out in outs:
@@ -451,6 +471,8 @@
             vmem((3, OWN, hd), F32),
             vmem((3, OWN, hd), F32),
             vmem((3, OWN, hd), F32),
+            vmem((OWN, hd), F32),
+            vmem((OWN, hd), F32),
             vmem((2, rows, hd), F32),
             vmem((keys, rows), F32),
             vmem((keys, HEADS * rows), F32),

time: 55.8 us -> 56 us (level)
  no operation moved by 1% of the time
where the time goes in v5:
time: 56 us; the launch traced here: 55.7 us
  Pallas kernels  55.1 us (98%)
  between operations  0.64 us (1%)
    pallas_call x1, Pallas kernels, body(): pl.pallas_call(functools.partial(kernel, ctx, roll), out_shape=(shape((HE...  53.2 us
    pallas_call x1, Pallas kernels, body(): pl.pallas_call(hand_over, out_shape=shapes, in_specs=[anywhere] * 6, out_...  1.83 us

profile of v5, /device:TPU:1, one launch (start us, length us, event | category | flops | bytes accessed | tf_op | source)
XLA Modules:
  0.0 55.7 jit_solution(5789712687264460858)
XLA Ops:
  0.6 53.2 %shard_map.145 = (bf16[768,128]{1,0:T(8,128)(2,1)}, bf16[128,256]{1,0:T(8,128)(2,1)}, f32[16,128]{1,0:T(8,128)}, f32[16,128]{1,0:T(8,128)}, f32[16,128]{1,0:T(8,128)}, /*index=5*/bf16[16,16,128]{2,1,0:T(8,128)(2,1)}) custom-call(s32[32]{0:T(128)} %order_hbm.1, s32[32,128]{1,0:T(8,128)} %bitcast.4, bf16[32,16,16,128]{3,2,1,0:T(8,128)(2,1)} %bitcast.3, ...), custom_call_target="tpu_custom_call" | custom-call | tf_op jit(solution)/shard_map/pallas_call | solution.py:458
  53.9 1.8 %shard_map.146 = (bf16[128,768]{1,0:T(8,128)(2,1)}, bf16[128,256]{1,0:T(8,128)(2,1)}, f32[16,128]{1,0:T(8,128)}, f32[16,128]{1,0:T(8,128)}, f32[16,128]{1,0:T(8,128)}, /*index=5*/bf16[16,16,128]{2,1,0:T(8,128)(2,1)}) custom-call(bf16[768,128]{1,0:T(8,128)(2,1)} %get-tuple-element.18.refs_0_, bf16[128,256]{1,0:T(8,128)(2,1)} %get-tuple-element.19.refs_1_, ...), custom_call_target="tpu_custom_call" | custom-call | tf_op jit(solution)/shard_map/pallas_call | solution.py:517

commit v6 on v4

--- a/solution.py
+++ b/solution.py
@@ -394,25 +394,22 @@
 def hand_over(*refs):
     sources, places, held, sem = refs[:6], refs[6:12], refs[12:18], refs[18]
     rows, hd = places[0].shape[0], sources[0].shape[1]
-    pairs = [(i, src, held[i]) for i, src in enumerate(sources)][1:]
-    pairs += [
-        (0, sources[0].at[pl.ds(h * rows, rows)], held[0].at[:, pl.ds(h * hd, hd)])
-        for h in range(HEADS)
-    ]
+    moves = []
+    for h in range(HEADS):
+        span = pl.ds(h * rows, rows)
+        moves.append((sources[0].at[span], held[0].at[span], places[0].at[:, pl.ds(h * hd, hd)]))
+    moves += list(zip(sources[1:], held[1:], places[1:]))
     fetches = [
-        (i, pltpu.make_async_copy(src, dst, sem.at[0, n])) for n, (i, src, dst) in enumerate(pairs)
+        pltpu.make_async_copy(src, mid, sem.at[0, n]) for n, (src, mid, _) in enumerate(moves)
     ]
     writes = [
-        pltpu.make_async_copy(src, dst, sem.at[1, i])
-        for i, (src, dst) in enumerate(zip(held, places))
+        pltpu.make_async_copy(mid, dst, sem.at[1, n]) for n, (_, mid, dst) in enumerate(moves)
     ]
-    for _, fetch in fetches:
+    for fetch in fetches:
         fetch.start()
-    for i, fetch in fetches:
+    for fetch, write in zip(fetches, writes):
         fetch.wait()
-        if i > 0:
-            writes[i].start()
-    writes[0].start()
+        write.start()
     for write in writes:
         write.wait()
 
@@ -497,7 +494,11 @@
         out_shape=shapes,
         in_specs=[anywhere] * 6,
         out_specs=[anywhere] * 6,
-        scratch_shapes=[*(vmem(s.shape, s.dtype) for s in shapes), pltpu.SemaphoreType.DMA((2, 11))],
+        scratch_shapes=[
+            vmem((HEADS * rows, hd), BF),
+            *(vmem(s.shape, s.dtype) for s in shapes[1:]),
+            pltpu.SemaphoreType.DMA((2, 11)),
+        ],
     )(*made)
     return (
         query_grad,

time: 55.8 us -> 55.8 us (level)
  no operation moved by 1% of the time
where the time goes in v6:
time: 55.8 us; the launch traced here: 55.6 us
  Pallas kernels  54.9 us (98%)
  between operations  0.64 us (1%)
    pallas_call x1, Pallas kernels, body(): pl.pallas_call(functools.partial(kernel, ctx, roll), out_shape=(shape((HE...  53.1 us
    pallas_call x1, Pallas kernels, body(): pl.pallas_call(hand_over, out_shape=shapes, in_specs=[anywhere] * 6, out_...  1.84 us

profile of v6, /device:TPU:1, one launch (start us, length us, event | category | flops | bytes accessed | tf_op | source)
XLA Modules:
  0.0 55.6 jit_solution(17820759991584482731)
XLA Ops:
  0.6 53.1 %shard_map.145 = (bf16[768,128]{1,0:T(8,128)(2,1)}, bf16[128,256]{1,0:T(8,128)(2,1)}, f32[16,128]{1,0:T(8,128)}, f32[16,128]{1,0:T(8,128)}, f32[16,128]{1,0:T(8,128)}, /*index=5*/bf16[16,16,128]{2,1,0:T(8,128)(2,1)}) custom-call(s32[32]{0:T(128)} %order_hbm.1, s32[32,128]{1,0:T(8,128)} %bitcast.4, bf16[32,16,16,128]{3,2,1,0:T(8,128)(2,1)} %bitcast.3, ...), custom_call_target="tpu_custom_call" | custom-call | tf_op jit(solution)/shard_map/pallas_call | solution.py:435
  53.7 1.8 %shard_map.146 = (bf16[128,768]{1,0:T(8,128)(2,1)}, bf16[128,256]{1,0:T(8,128)(2,1)}, f32[16,128]{1,0:T(8,128)}, f32[16,128]{1,0:T(8,128)}, f32[16,128]{1,0:T(8,128)}, /*index=5*/bf16[16,16,128]{2,1,0:T(8,128)(2,1)}) custom-call(bf16[768,128]{1,0:T(8,128)(2,1)} %get-tuple-element.18.refs_0_, bf16[128,256]{1,0:T(8,128)(2,1)} %get-tuple-element.19.refs_1_, ...), custom_call_target="tpu_custom_call" | custom-call | tf_op jit(solution)/shard_map/pallas_call | solution.py:492
